TPU v7x, 512 devices: a whole 4x8x8 slice. The times are simulated.
512 devices in a mesh: section: 4 (over y_hi, core), dp: 8 (over z), tensor: 16 (over x, y_lo).
Axes of the slice: x: 4, y: 8 (y_hi: 2, y_lo: 4; y = y_hi * 4 + y_lo), z: 8, core: 2. Of those that a mesh axis runs over, the one named last changes fastest.
Arguments:
- saved_input: bfloat16 [4, 256, 8192], P('section', 'dp', 'tensor'), may hold values from -6 to 6
- w_up: bfloat16 [4, 8192, 16384], P('section', 'tensor', 'dp'), may hold values from -0.0625 to 0.0625
- w_down: bfloat16 [4, 16384, 8192], P('section', 'dp', 'tensor'), may hold values from -0.046875 to 0.046875
- sent_grad: bfloat16 [4, 256, 8192], P('section', ('dp', 'tensor')), may hold values from -6 to 6
Outputs:
- input_grad: bfloat16 [4, 256, 8192], P('section', 'dp', 'tensor')
All inputs are finite; a program needn't handle non-finite values.
Results may differ from a plain program's by a relative error of at most 0.02.
Values may be sent and summed in bfloat16 or wider, within the bound.
No kernel may reach another device: no remote copies, remote signals or barrier semaphores. Data moves between devices by JAX's collectives and lax.ppermute only.
A program may use at most 64 MiB of HBM per device.

v0:
```python
import jax
import jax.numpy as jnp
from jax import lax
from jax.sharding import PartitionSpec as P


def shifted(value, axis, steps):
    count = lax.axis_size(axis)
    pairs = [(source, (source + steps) % count) for source in range(count)]
    return lax.ppermute(value, axis, pairs)


def gelu_slope(value):
    coeff = 0.7978845608028654
    inner = coeff * (value + 0.044715 * value * value * value)
    tangent = jnp.tanh(inner)
    return 0.5 * (1.0 + tangent) + 0.5 * value * (1.0 - tangent * tangent) * coeff * (
        1.0 + 3.0 * 0.044715 * value * value
    )


def per_device(saved_input, w_up, w_down, sent_grad):
    tokens_in = saved_input[0]
    up_block = w_up[0]
    down_block = w_down[0]
    contract_last = (((1,), (1,)), ((), ()))
    moved = shifted(sent_grad[0], "section", -1)
    local_grad = lax.all_to_all(moved, "tensor", split_axis=1, concat_axis=0, tiled=True)
    back_part = lax.dot_general(
        lax.all_gather(local_grad, "dp", axis=0, tiled=True),
        down_block,
        contract_last,
        preferred_element_type=jnp.float32,
    )
    hidden_part = jnp.dot(
        lax.all_gather(tokens_in, "dp", axis=0, tiled=True),
        up_block,
        preferred_element_type=jnp.float32,
    )
    hidden, back_hidden = (
        lax.psum(hidden_part.astype(jnp.bfloat16), "tensor").astype(jnp.float32),
        lax.psum(back_part.astype(jnp.bfloat16), "tensor").astype(jnp.float32),
    )
    slope_grad = (back_hidden * gelu_slope(hidden)).astype(jnp.bfloat16)
    summed = lax.psum_scatter(
        lax.dot_general(
            slope_grad, up_block, contract_last, preferred_element_type=jnp.float32
        ).astype(jnp.bfloat16),
        "dp",
        scatter_dimension=0,
        tiled=True,
    ).astype(jnp.float32)
    result = (local_grad.astype(jnp.float32) + summed).astype(jnp.bfloat16)
    return result[None]


def solution(mesh):
    in_specs = (
        P("section", "dp", "tensor"),
        P("section", "tensor", "dp"),
        P("section", "dp", "tensor"),
        P("section", ("dp", "tensor"), None),
    )
    out_specs = P("section", "dp", "tensor")
    return jax.shard_map(
        per_device, mesh=mesh, in_specs=in_specs, out_specs=out_specs, check_vma=False
    )
```

profile of v0, /device:TPU:6, one launch (start us, length us, event | category | flops | bytes accessed | tf_op | source)
XLA Modules:
  0.0 312.3 jit_solution(9172371081115765656)
XLA Ops:
  6.5 0.0 copy-start
  6.5 7.3 %collective-permute-start = (bf16[2,8192]{1,0:T(2,128)(2,1)}, bf16[2,8192]{1,0:T(2,128)(2,1)}, u32[]{:S(2)}, u32[]{:S(2)}) collective-permute-start(bf16[2,8192]{1,0:T(2,128)(2,1)} %bitcast.20), channel_id=1, source_target_pairs={{0,384},{128,0},{256,128},{384,256},{1,385},{129,1},{257,129},{385... | collective-permute-start | bytes 98312 | tf_op jit(solution)/shard_map/ppermute | solution.py:10
  13.8 31.4 %all-gather = bf16[1,256,512]{2,1,0:T(8,128)(2,1)S(1)} all-gather(bf16[1,32,512]{2,1,0:T(8,128)(2,1)} %param.4), channel_id=2, replica_groups=mesh['section'=4,'dp'=8,'tensor'=16] {'dp'}, dimensions={1}, use_global_device_ids=true | all-gather | bytes 294912 | tf_op jit(solution)/shard_map/all_gather | solution.py:36
  45.2 0.0 collective-permute-done
  45.2 5.2 %all-to-all-start = ((bf16[2,16,512]{2,0,1:T(2,128)(2,1)}), bf16[2,16,512]{2,0,1:T(2,128)(2,1)S(1)}, u32[]{:S(2)}, u32[]{:S(2)}) async-start(bf16[2,16,512]{2,0,1:T(2,128)(2,1)} %bitcast.1), calls=%async_computation | async-start | bytes 65536 | tf_op jit(solution)/shard_map/all_to_all | solution.py:28
  50.4 0.0 all-reduce.3.cloned.1.call-start
  50.5 0.0 copy-done
  50.5 1.7 convolution_convert_fusion
  52.2 4.3 %all-to-all-done = bf16[2,16,512]{2,0,1:T(2,128)(2,1)S(1)} async-done(((bf16[2,16,512]{2,0,1:T(2,128)(2,1)}), bf16[2,16,512]{2,0,1:T(2,128)(2,1)S(1)}, u32[]{:S(2)}, u32[]{:S(2)}) %all-to-all-start) | async-done | bytes 32800 | tf_op jit(solution)/shard_map/all_to_all | solution.py:28
  56.5 24.8 %all_gather.6 = bf16[256,512]{1,0:T(8,128)(2,1)S(1)} all-gather(bf16[32,512]{1,0:T(8,128)(2,1)S(1)} %all_to_all.17), channel_id=1, replica_groups=mesh['section'=4,'dp'=8,'tensor'=16] {'dp'}, dimensions={0}, use_global_device_ids=true | all-gather | bytes 294912 | tf_op jit(solution)/shard_map/all_gather | solution.py:30
  81.3 3.3 %convolution_convert_fusion.1 = bf16[256,2048]{1,0:T(8,128)(2,1)} fusion(bf16[256,512]{1,0:T(8,128)(2,1)S(1)} %all_gather.6, bf16[1,2048,512]{2,1,0:T(8,128)(2,1)} %param.6), kind=kOutput, calls=%fused_computation.8 | convolution fusion | flops 537395200 | bytes 3407872 | tf_op jit(solution)/shard_map/dot_general | solution.py:29
  84.6 0.0 all-reduce.3.cloned.1.call-update
  84.6 0.0 reduce-scatter.2.cloned.1.call-start
  84.7 170.7 %all-reduce.3.cloned.1.call-done = (bf16[256,2048]{1,0:T(8,128)(2,1)}, bf16[256,2048]{1,0:T(8,128)(2,1)}) async-done(((bf16[256,2048]{1,0:T(8,128)(2,1)}, bf16[256,2048]{1,0:T(8,128)(2,1)}), (bf16[256,2048]{1,0:T(8,128)(2,1)}, bf16[256,2048]{1,0:T(8,128)(2,1)})) %all-reduce.3.cloned.1.call-update) | async-done | bytes 2097168 | tf_op jit(solution)/shard_map/psum | solution.py:41
  255.4 3.9 %fusion.13 = bf16[256,512]{1,0:T(8,128)(2,1)} fusion(bf16[1,512,2048]{2,1,0:T(8,128)(2,1)S(1)} %copy-done, bf16[256,2048]{1,0:T(8,128)(2,1)} %get-tuple-element.5, bf16[256,2048]{1,0:T(8,128)(2,1)} %get-tuple-element.6), kind=kOutput, calls=%fused_computation.22 | convolution fusion | flops 548012032 | bytes 4456448 | tf_op jit(solution)/shard_map/dot_general | solution.py:46
  259.3 0.0 reduce-scatter.2.cloned.1.call-update
  259.3 44.8 %reduce-scatter.2.cloned.1.call-done = bf16[32,512]{1,0:T(8,128)(2,1)} async-done(((bf16[256,512]{1,0:T(8,128)(2,1)}), bf16[32,512]{1,0:T(8,128)(2,1)}) %reduce-scatter.2.cloned.1.call-update) | async-done | bytes 32784 | tf_op jit(solution)/shard_map/reduce_scatter | solution.py:45
  304.1 1.4 fusion.23
  (1 shorter events, 0.0 us)
Async XLA Ops:
  6.5 43.9 %copy-start = (bf16[1,512,2048]{2,1,0:T(8,128)(2,1)S(1)}, bf16[1,512,2048]{2,1,0:T(8,128)(2,1)}, u32[]{:S(2)}) copy-start(bf16[1,512,2048]{2,1,0:T(8,128)(2,1)} %param.5) | copy-start | bytes 6291460
  6.5 38.7 %collective-permute-start = (bf16[2,8192]{1,0:T(2,128)(2,1)}, bf16[2,8192]{1,0:T(2,128)(2,1)}, u32[]{:S(2)}, u32[]{:S(2)}) collective-permute-start(bf16[2,8192]{1,0:T(2,128)(2,1)} %bitcast.20), channel_id=1, source_target_pairs={{0,384},{128,0},{256,128},{384,256},{1,385},{129,1},{257,129},{385... | collective-permute-start | bytes 98312 | tf_op jit(solution)/shard_map/ppermute | solution.py:10
  45.2 11.2 %all-to-all-start = ((bf16[2,16,512]{2,0,1:T(2,128)(2,1)}), bf16[2,16,512]{2,0,1:T(2,128)(2,1)S(1)}, u32[]{:S(2)}, u32[]{:S(2)}) async-start(bf16[2,16,512]{2,0,1:T(2,128)(2,1)} %bitcast.1), calls=%async_computation | async-start | bytes 65536 | tf_op jit(solution)/shard_map/all_to_all | solution.py:28
  50.4 205.0 %all-reduce.3.cloned.1.call-start = ((), (), s32[]{:S(2)}) async-start(), calls=%async_computation.3 | async-start | bytes 4194304 | tf_op jit(solution)/shard_map/psum | solution.py:41
  84.6 219.5 %reduce-scatter.2.cloned.1.call-start = ((), (), s32[]{:S(2)}) async-start(), calls=%async_computation.2 | async-start | bytes 294912 | tf_op jit(solution)/shard_map/reduce_scatter | solution.py:45
Sparse Core Ops, SparseCore 0:
  84.7 170.6 all-reduce.2
  259.5 44.6 reduce-scatter.1
where the time goes:
time: 313 us; the launch traced here: 312 us
  waiting for transfers between devices  220 us (70%)
  blocking collectives  56.2 us (18%)
  between operations  13.4 us (4%)
  starting transfers between devices  12.6 us (4%)
  matrix products  8.97 us (3%)
    psum x1, waiting for transfers between devices, per_device(): lax.psum(hidden_part.astype(jnp.bfloat16), 'tensor').astype(jnp.float32)  171 us
    reduce_scatter x1, waiting for transfers between devices, per_device(): lax.psum_scatter(lax.dot_general(slope_grad, up_block, contract_last, pre...  44.8 us
    all_gather x1, blocking collectives, per_device(): lax.all_gather(tokens_in, 'dp', axis=0, tiled=True)  31.4 us
    all_gather x1, blocking collectives, per_device(): lax.all_gather(local_grad, 'dp', axis=0, tiled=True)  24.8 us
    ppermute x1, starting transfers between devices, shifted(): return lax.ppermute(value, axis, pairs)  7.29 us
  transfers between devices with their start and end apart: 4, of which 3 were waited for; matrix products, arithmetic and copies ran while one was open for 1% of the time, Pallas kernels for 0%

commit v1 on v0

v1 whole, which is shorter than its diff:
```python
import jax
import jax.numpy as jnp
from jax import lax
from jax.sharding import Mesh
from jax.sharding import PartitionSpec as P

TENSOR = ("tx", "ty")


def shifted(value, axis, steps):
    count = lax.axis_size(axis)
    pairs = [(source, (source + steps) % count) for source in range(count)]
    return lax.ppermute(value, axis, pairs)


def gathered(value, axis):
    count = lax.axis_size(axis)
    copies = jnp.broadcast_to(value[None], (count,) + value.shape)
    parts = lax.all_to_all(copies, axis, split_axis=0, concat_axis=0, tiled=True)
    return parts.reshape((count * value.shape[0],) + value.shape[1:])


def scattered_sum(value, axis):
    count = lax.axis_size(axis)
    split = value.reshape((count, value.shape[0] // count) + value.shape[1:])
    parts = lax.all_to_all(split, axis, split_axis=0, concat_axis=0, tiled=True)
    return jnp.sum(parts.astype(jnp.float32), axis=0)


def tensor_sum(part):
    across_x = scattered_sum(part.astype(jnp.bfloat16), "tx")
    return scattered_sum(across_x.astype(jnp.bfloat16), "ty")


def gelu_slope(value):
    coeff = 0.7978845608028654
    inner = coeff * (value + 0.044715 * value * value * value)
    tangent = jnp.tanh(inner)
    return 0.5 * (1.0 + tangent) + 0.5 * value * (1.0 - tangent * tangent) * coeff * (
        1.0 + 3.0 * 0.044715 * value * value
    )


def per_device(saved_input, w_up, w_down, sent_grad):
    tokens_in = saved_input[0]
    up_block = w_up[0]
    down_block = w_down[0]
    contract_last = (((1,), (1,)), ((), ()))
    moved = shifted(sent_grad[0], "section", -1)
    local_grad = lax.all_to_all(moved, TENSOR, split_axis=1, concat_axis=0, tiled=True)
    hidden_part = jnp.dot(
        gathered(tokens_in, "dp"), up_block, preferred_element_type=jnp.float32
    )
    hidden = tensor_sum(hidden_part)
    back_part = lax.dot_general(
        gathered(local_grad, "dp"),
        down_block,
        contract_last,
        preferred_element_type=jnp.float32,
    )
    back_hidden = tensor_sum(back_part)
    slope_grad = (back_hidden * gelu_slope(hidden)).astype(jnp.bfloat16)
    slope_grad = gathered(gathered(slope_grad, "ty"), "tx")
    branch = lax.dot_general(
        slope_grad, up_block, contract_last, preferred_element_type=jnp.float32
    )
    summed = scattered_sum(branch.astype(jnp.bfloat16), "dp")
    result = (local_grad.astype(jnp.float32) + summed).astype(jnp.bfloat16)
    return result[None]


def solution(mesh):
    count_y = 4
    sizes = (
        mesh.shape["section"],
        mesh.shape["dp"],
        mesh.shape["tensor"] // count_y,
        count_y,
    )
    fine = Mesh(mesh.devices.reshape(sizes), ("section", "dp") + TENSOR)
    in_specs = (
        P("section", "dp", TENSOR),
        P("section", TENSOR, "dp"),
        P("section", "dp", TENSOR),
        P("section", ("dp",) + TENSOR, None),
    )
    out_specs = P("section", "dp", TENSOR)
    return jax.shard_map(
        per_device, mesh=fine, in_specs=in_specs, out_specs=out_specs, check_vma=False
    )
```

time: 313 us -> 162 us (0.52)
  waiting for transfers between devices: 220 us -> 69.5 us
  starting transfers between devices: 12.6 us -> 42.4 us
  blocking collectives: 56.2 us -> 34.6 us
  between operations: 13.4 us -> 0.11 us
  local copies, waits for them, and re-layouts: 0.02 us -> 3.39 us
    psum x1 -> x0, waiting for transfers between devices: 171 us -> none  [per_device(): lax.psum(hidden_part.astype(jnp.bfloat16), 'tensor').astype(jnp.float32)]
    all_to_all x1 -> x7, waiting for transfers between devices: 4.26 us -> 67.6 us  [the longest x5 43.7 us: scattered_sum(): parts = lax.all_to_all(split, axis, split_axis=0, concat_axis=0, tiled=True)]
    all_gather x2 -> x0, blocking collectives: 56.2 us -> none  [the longest x1 31.4 us: per_device(): lax.all_gather(tokens_in, 'dp', axis=0, tiled=True)]
    reduce_scatter x1 -> x0, waiting for transfers between devices: 44.8 us -> none  [per_device(): lax.psum_scatter(lax.dot_general(slope_grad, up_block, contract_last, pre...]
    all_to_all x0 -> x3, blocking collectives: none -> 34.6 us  [the longest x2 23.7 us: gathered(): lax.all_to_all(copies, axis, split_axis=0, concat_axis=0, tiled=True)]
    all_to_all x1 -> x7, starting transfers between devices: 5.21 us -> 35.1 us  [the longest x5 21.3 us: scattered_sum(): parts = lax.all_to_all(split, axis, split_axis=0, concat_axis=0, tiled=True)]
    reduce_sum x0 -> x5, other arithmetic: none -> 3.19 us  [scattered_sum(): return jnp.sum(parts.astype(jnp.float32), axis=0)]
  transfers between devices with their start and end apart: 4 -> 8, of which waited for: 3 -> 8; matrix products, arithmetic and copies ran while one was open for 1% -> 5% of each run, Pallas kernels for 0% -> 0%
where the time goes in v1:
time: 162 us; the launch traced here: 160 us
  waiting for transfers between devices  69.5 us (43%)
  starting transfers between devices  42.4 us (26%)
  blocking collectives  34.6 us (21%)
  matrix products  6.48 us (4%)
  other arithmetic  3.94 us (2%)
  local copies, waits for them, and re-layouts  3.39 us (2%)
    all_to_all x5, waiting for transfers between devices, scattered_sum(): parts = lax.all_to_all(split, axis, split_axis=0, concat_axis=0, tiled=True)  43.7 us
    all_to_all x2, waiting for transfers between devices, gathered(): lax.all_to_all(copies, axis, split_axis=0, concat_axis=0, tiled=True)  23.9 us
    all_to_all x2, blocking collectives, gathered(): lax.all_to_all(copies, axis, split_axis=0, concat_axis=0, tiled=True)  23.7 us
    all_to_all x5, starting transfers between devices, scattered_sum(): parts = lax.all_to_all(split, axis, split_axis=0, concat_axis=0, tiled=True)  21.3 us
    all_to_all x2, starting transfers between devices, gathered(): lax.all_to_all(copies, axis, split_axis=0, concat_axis=0, tiled=True)  13.7 us
    all_to_all x1, blocking collectives, per_device(): lax.all_to_all(moved, TENSOR, split_axis=1, concat_axis=0, tiled=True)  10.9 us
    ppermute x1, starting transfers between devices, shifted(): return lax.ppermute(value, axis, pairs)  7.29 us
    dot_general x1, matrix products, per_device(): lax.dot_general(gathered(local_grad, 'dp'), down_block, contract_last, pr...  3.31 us
  transfers between devices with their start and end apart: 8, of which 8 were waited for; matrix products, arithmetic and copies ran while one was open for 5% of the time, Pallas kernels for 0%

profile of v1, /device:TPU:6, one launch (start us, length us, event | category | flops | bytes accessed | tf_op | source)
XLA Modules:
  0.0 160.4 jit_solution(13384121365030408034)
XLA Ops:
  0.0 0.0 copy-start
  0.0 7.3 %collective-permute-start = (bf16[2,8192]{1,0:T(2,128)(2,1)}, bf16[2,8192]{1,0:T(2,128)(2,1)S(1)}, u32[]{:S(2)}, u32[]{:S(2)}) collective-permute-start(bf16[2,8192]{1,0:T(2,128)(2,1)} %bitcast.40), channel_id=1, source_target_pairs={{0,384},{128,0},{256,128},{384,256},{1,385},{129,1},{257,129},{385... | collective-permute-start | bytes 98312 | tf_op jit(solution)/shard_map/ppermute | solution.py:13
  7.3 1.9 %collective-permute-done = bf16[2,8192]{1,0:T(2,128)(2,1)S(1)} collective-permute-done((bf16[2,8192]{1,0:T(2,128)(2,1)}, bf16[2,8192]{1,0:T(2,128)(2,1)S(1)}, u32[]{:S(2)}, u32[]{:S(2)}) %collective-permute-start) | collective-permute-done | bytes 32800 | tf_op jit(solution)/shard_map/ppermute | solution.py:13
  9.2 10.9 %all_to_all.61 = bf16[2,16,512]{2,0,1:T(2,128)(2,1)S(1)} all-to-all(bf16[2,16,512]{2,0,1:T(2,128)(2,1)S(1)} %bitcast.39), channel_id=1, replica_groups=mesh['section'=4,'dp'=8,'tx'=4,'ty'=4] {'tx','ty'}, dimensions={1} | all-to-all | bytes 65536 | tf_op jit(solution)/shard_map/all_to_all | solution.py:50
  20.1 1.5 broadcast_in_dim.32
  21.6 10.3 %all-to-all-start.4 = ((bf16[8,32,512]{2,1,0:T(8,128)(2,1)}), bf16[8,32,512]{2,1,0:T(8,128)(2,1)S(1)}, u32[]{:S(2)}, u32[]{:S(2)}) async-start(bf16[8,32,512]{2,1,0:T(8,128)(2,1)} %broadcast_in_dim.32), calls=%async_computation.4 | async-start | bytes 524288 | tf_op jit(solution)/shard_map/all_to_all | solution.py:19
  31.9 13.3 %all-to-all-done.4 = bf16[8,32,512]{2,1,0:T(8,128)(2,1)S(1)} async-done(((bf16[8,32,512]{2,1,0:T(8,128)(2,1)}), bf16[8,32,512]{2,1,0:T(8,128)(2,1)S(1)}, u32[]{:S(2)}, u32[]{:S(2)}) %all-to-all-start.4) | async-done | bytes 262176 | tf_op jit(solution)/shard_map/all_to_all | solution.py:19
  45.2 0.7 broadcast_in_dim.30
  45.9 3.4 %all-to-all-start.1 = ((bf16[8,32,512]{2,1,0:T(8,128)(2,1)}), bf16[8,32,512]{2,1,0:T(8,128)(2,1)S(1)}, u32[]{:S(2)}, u32[]{:S(2)}) async-start(bf16[8,32,512]{2,1,0:T(8,128)(2,1)} %broadcast_in_dim.30), calls=%async_computation.1 | async-start | bytes 524288 | tf_op jit(solution)/shard_map/all_to_all | solution.py:19
  49.3 0.0 copy-done
  49.3 1.7 %convolution_convert_fusion = bf16[256,2048]{1,0:T(8,128)(2,1)} fusion(bf16[256,512]{1,0:T(8,128)(2,1)S(1)} %bitcast.35, bf16[1,512,2048]{2,1,0:T(8,128)(2,1)S(1)} %copy-done), kind=kOutput, calls=%fused_computation | convolution fusion | flops 537395200 | bytes 3407872 | tf_op jit(solution)/shard_map/dot_general | solution.py:51
  51.1 10.6 %all-to-all-done.1 = bf16[8,32,512]{2,1,0:T(8,128)(2,1)S(1)} async-done(((bf16[8,32,512]{2,1,0:T(8,128)(2,1)}), bf16[8,32,512]{2,1,0:T(8,128)(2,1)S(1)}, u32[]{:S(2)}, u32[]{:S(2)}) %all-to-all-start.1) | async-done | bytes 262176 | tf_op jit(solution)/shard_map/all_to_all | solution.py:19
  61.7 5.6 %all-to-all-start.5 = ((bf16[4,64,2048]{2,1,0:T(8,128)(2,1)}), bf16[4,64,2048]{2,1,0:T(8,128)(2,1)S(1)}, u32[]{:S(2)}, u32[]{:S(2)}) async-start(bf16[4,64,2048]{2,1,0:T(8,128)(2,1)} %bitcast.31), calls=%async_computation.5 | async-start | bytes 2097152 | tf_op jit(solution)/shard_map/all_to_all | solution.py:26
  67.2 3.3 %convolution_convert_fusion.1 = bf16[256,2048]{1,0:T(8,128)(2,1)} fusion(bf16[256,512]{1,0:T(8,128)(2,1)S(1)} %bitcast.36, bf16[1,2048,512]{2,1,0:T(8,128)(2,1)} %param.6), kind=kOutput, calls=%fused_computation.1 | convolution fusion | flops 537395200 | bytes 3407872 | tf_op jit(solution)/shard_map/dot_general | solution.py:55
  70.5 10.2 %all-to-all-done.5 = bf16[4,64,2048]{2,1,0:T(8,128)(2,1)S(1)} async-done(((bf16[4,64,2048]{2,1,0:T(8,128)(2,1)}), bf16[4,64,2048]{2,1,0:T(8,128)(2,1)S(1)}, u32[]{:S(2)}, u32[]{:S(2)}) %all-to-all-start.5) | async-done | bytes 1048608 | tf_op jit(solution)/shard_map/all_to_all | solution.py:26
  80.7 0.0 copy-start.1
  80.7 1.0 copy-done.1
  81.7 5.6 %all-to-all-start.2 = ((bf16[4,64,2048]{2,1,0:T(8,128)(2,1)}), bf16[4,64,2048]{2,1,0:T(8,128)(2,1)S(1)}, u32[]{:S(2)}, u32[]{:S(2)}) async-start(bf16[4,64,2048]{2,1,0:T(8,128)(2,1)} %bitcast.32), calls=%async_computation.2 | async-start | bytes 2097152 | tf_op jit(solution)/shard_map/all_to_all | solution.py:26
  87.3 2.2 %reduce_sum.55 = bf16[64,2048]{1,0:T(8,128)(2,1)} reduce(bf16[4,64,2048]{2,1,0:T(8,128)(2,1)} %copy-done.1, bf16[]{:T(256)} %constant.2.clone.1), dimensions={0}, to_apply=%region_2.0 | reduce | flops 393216 | bytes 1310722 | tf_op jit(solution)/shard_map/reduce_sum | solution.py:27
  89.5 10.4 %all-to-all-done.2 = bf16[4,64,2048]{2,1,0:T(8,128)(2,1)S(1)} async-done(((bf16[4,64,2048]{2,1,0:T(8,128)(2,1)}), bf16[4,64,2048]{2,1,0:T(8,128)(2,1)S(1)}, u32[]{:S(2)}, u32[]{:S(2)}) %all-to-all-start.2) | async-done | bytes 1048608 | tf_op jit(solution)/shard_map/all_to_all | solution.py:26
  99.9 3.4 %all-to-all-start.6 = ((bf16[4,16,2048]{2,1,0:T(8,128)(2,1)}), bf16[4,16,2048]{2,1,0:T(8,128)(2,1)S(1)}, u32[]{:S(2)}, u32[]{:S(2)}) async-start(bf16[4,16,2048]{2,1,0:T(8,128)(2,1)} %bitcast.11), calls=%async_computation.6 | async-start | bytes 524288 | tf_op jit(solution)/shard_map/all_to_all | solution.py:26
  103.3 0.9 reduce_sum.53
  104.2 6.1 %all-to-all-done.6 = bf16[4,16,2048]{2,1,0:T(8,128)(2,1)S(1)} async-done(((bf16[4,16,2048]{2,1,0:T(8,128)(2,1)}), bf16[4,16,2048]{2,1,0:T(8,128)(2,1)S(1)}, u32[]{:S(2)}, u32[]{:S(2)}) %all-to-all-start.6) | async-done | bytes 262176 | tf_op jit(solution)/shard_map/all_to_all | solution.py:26
  110.4 3.4 %all-to-all-start.3 = ((bf16[4,16,2048]{2,1,0:T(8,128)(2,1)}), bf16[4,16,2048]{2,1,0:T(8,128)(2,1)S(1)}, u32[]{:S(2)}, u32[]{:S(2)}) async-start(bf16[4,16,2048]{2,1,0:T(8,128)(2,1)} %bitcast.6), calls=%async_computation.3 | async-start | bytes 524288 | tf_op jit(solution)/shard_map/all_to_all | solution.py:26
  113.8 6.7 %all-to-all-done.3 = bf16[4,16,2048]{2,1,0:T(8,128)(2,1)S(1)} async-done(((bf16[4,16,2048]{2,1,0:T(8,128)(2,1)}), bf16[4,16,2048]{2,1,0:T(8,128)(2,1)S(1)}, u32[]{:S(2)}, u32[]{:S(2)}) %all-to-all-start.3) | async-done | bytes 262176 | tf_op jit(solution)/shard_map/all_to_all | solution.py:26
  120.6 0.1 fusion.13
  120.7 10.4 %all_to_all.62 = bf16[4,16,2048]{2,1,0:T(8,128)(2,1)S(1)} all-to-all(bf16[4,16,2048]{2,1,0:T(8,128)(2,1)S(1)} %broadcast_in_dim.33), channel_id=1, replica_groups=mesh['section'=4,'dp'=8,'tx'=4,'ty'=4] {'ty'}, dimensions={0} | all-to-all | bytes 524288 | tf_op jit(solution)/shard_map/all_to_all | solution.py:19
  131.0 0.1 broadcast_in_dim.35
  131.2 13.3 %all_to_all.63 = bf16[4,64,2048]{2,1,0:T(8,128)(2,1)S(1)} all-to-all(bf16[4,64,2048]{2,1,0:T(8,128)(2,1)S(1)} %broadcast_in_dim.35), channel_id=1, replica_groups=mesh['section'=4,'dp'=8,'tx'=4,'ty'=4] {'tx'}, dimensions={0} | all-to-all | bytes 2097152 | tf_op jit(solution)/shard_map/all_to_all | solution.py:19
  144.5 1.4 fusion.4
  145.9 3.4 %all-to-all-start.9 = ((bf16[8,32,512]{2,1,0:T(8,128)(2,1)}), bf16[8,32,512]{2,1,0:T(8,128)(2,1)S(1)}, u32[]{:S(2)}, u32[]{:S(2)}) async-start(bf16[8,32,512]{2,1,0:T(8,128)(2,1)} %bitcast.14), calls=%async_computation.9 | async-start | bytes 524288 | tf_op jit(solution)/shard_map/all_to_all | solution.py:26
  149.4 10.3 %all-to-all-done.9 = bf16[8,32,512]{2,1,0:T(8,128)(2,1)S(1)} async-done(((bf16[8,32,512]{2,1,0:T(8,128)(2,1)}), bf16[8,32,512]{2,1,0:T(8,128)(2,1)S(1)}, u32[]{:S(2)}, u32[]{:S(2)}) %all-to-all-start.9) | async-done | bytes 262176 | tf_op jit(solution)/shard_map/all_to_all | solution.py:26
  159.8 0.6 fusion.14
  (7 shorter events, 0.2 us)
Async XLA Ops:
  0.0 49.3 %copy-start = (bf16[1,512,2048]{2,1,0:T(8,128)(2,1)S(1)}, bf16[1,512,2048]{2,1,0:T(8,128)(2,1)}, u32[]{:S(2)}) copy-start(bf16[1,512,2048]{2,1,0:T(8,128)(2,1)} %param.5) | copy-start | bytes 6291460
  0.0 9.2 %collective-permute-start = (bf16[2,8192]{1,0:T(2,128)(2,1)}, bf16[2,8192]{1,0:T(2,128)(2,1)S(1)}, u32[]{:S(2)}, u32[]{:S(2)}) collective-permute-start(bf16[2,8192]{1,0:T(2,128)(2,1)} %bitcast.40), channel_id=1, source_target_pairs={{0,384},{128,0},{256,128},{384,256},{1,385},{129,1},{257,129},{385... | collective-permute-start | bytes 98312 | tf_op jit(solution)/shard_map/ppermute | solution.py:13
  21.6 23.6 %all-to-all-start.4 = ((bf16[8,32,512]{2,1,0:T(8,128)(2,1)}), bf16[8,32,512]{2,1,0:T(8,128)(2,1)S(1)}, u32[]{:S(2)}, u32[]{:S(2)}) async-start(bf16[8,32,512]{2,1,0:T(8,128)(2,1)} %broadcast_in_dim.32), calls=%async_computation.4 | async-start | bytes 524288 | tf_op jit(solution)/shard_map/all_to_all | solution.py:19
  45.9 15.8 %all-to-all-start.1 = ((bf16[8,32,512]{2,1,0:T(8,128)(2,1)}), bf16[8,32,512]{2,1,0:T(8,128)(2,1)S(1)}, u32[]{:S(2)}, u32[]{:S(2)}) async-start(bf16[8,32,512]{2,1,0:T(8,128)(2,1)} %broadcast_in_dim.30), calls=%async_computation.1 | async-start | bytes 524288 | tf_op jit(solution)/shard_map/all_to_all | solution.py:19
  61.7 19.0 %all-to-all-start.5 = ((bf16[4,64,2048]{2,1,0:T(8,128)(2,1)}), bf16[4,64,2048]{2,1,0:T(8,128)(2,1)S(1)}, u32[]{:S(2)}, u32[]{:S(2)}) async-start(bf16[4,64,2048]{2,1,0:T(8,128)(2,1)} %bitcast.31), calls=%async_computation.5 | async-start | bytes 2097152 | tf_op jit(solution)/shard_map/all_to_all | solution.py:26
  80.7 1.0 copy-start.1
  81.7 18.2 %all-to-all-start.2 = ((bf16[4,64,2048]{2,1,0:T(8,128)(2,1)}), bf16[4,64,2048]{2,1,0:T(8,128)(2,1)S(1)}, u32[]{:S(2)}, u32[]{:S(2)}) async-start(bf16[4,64,2048]{2,1,0:T(8,128)(2,1)} %bitcast.32), calls=%async_computation.2 | async-start | bytes 2097152 | tf_op jit(solution)/shard_map/all_to_all | solution.py:26
  99.9 10.4 %all-to-all-start.6 = ((bf16[4,16,2048]{2,1,0:T(8,128)(2,1)}), bf16[4,16,2048]{2,1,0:T(8,128)(2,1)S(1)}, u32[]{:S(2)}, u32[]{:S(2)}) async-start(bf16[4,16,2048]{2,1,0:T(8,128)(2,1)} %bitcast.11), calls=%async_computation.6 | async-start | bytes 524288 | tf_op jit(solution)/shard_map/all_to_all | solution.py:26
  110.4 10.2 %all-to-all-start.3 = ((bf16[4,16,2048]{2,1,0:T(8,128)(2,1)}), bf16[4,16,2048]{2,1,0:T(8,128)(2,1)S(1)}, u32[]{:S(2)}, u32[]{:S(2)}) async-start(bf16[4,16,2048]{2,1,0:T(8,128)(2,1)} %bitcast.6), calls=%async_computation.3 | async-start | bytes 524288 | tf_op jit(solution)/shard_map/all_to_all | solution.py:26
  145.9 13.8 %all-to-all-start.9 = ((bf16[8,32,512]{2,1,0:T(8,128)(2,1)}), bf16[8,32,512]{2,1,0:T(8,128)(2,1)S(1)}, u32[]{:S(2)}, u32[]{:S(2)}) async-start(bf16[8,32,512]{2,1,0:T(8,128)(2,1)} %bitcast.14), calls=%async_computation.9 | async-start | bytes 524288 | tf_op jit(solution)/shard_map/all_to_all | solution.py:26

commit v2 on v1

v2 whole, which is shorter than its diff:
```python
import jax
import jax.numpy as jnp
from jax import lax
from jax.sharding import Mesh
from jax.sharding import PartitionSpec as P

TENSOR = ("tx", "ty1", "ty0")
NEAR = ("tx", "ty0")


def exchange(value, axis):
    return lax.all_to_all(value, axis, split_axis=0, concat_axis=0, tiled=True)


def copies(value, axis):
    return jnp.broadcast_to(value[None], (lax.axis_size(axis),) + value.shape)


def gelu_slope(value):
    coeff = 0.7978845608028654
    inner = coeff * (value + 0.044715 * value * value * value)
    tangent = jnp.tanh(inner)
    return 0.5 * (1.0 + tangent) + 0.5 * value * (1.0 - tangent * tangent) * coeff * (
        1.0 + 3.0 * 0.044715 * value * value
    )


def previous_section_grad(sent):
    sections, parts = lax.axis_size("section"), lax.axis_size(TENSOR)
    tokens, width = sent.shape
    here = lax.axis_index("section")
    blocks = sent.reshape(tokens, parts, width // parts).transpose(1, 0, 2)
    slots = lax.broadcasted_iota(jnp.int32, (sections, 1, 1, 1), 0)
    blocks = jnp.where(slots == (here + sections - 1) % sections, blocks[None], 0)
    blocks = blocks.reshape((sections * parts,) + blocks.shape[2:])
    blocks = exchange(blocks, ("section",) + TENSOR)
    blocks = blocks.reshape(sections, parts * tokens, width // parts)
    return lax.dynamic_index_in_dim(
        blocks, (here + 1) % sections, axis=0, keepdims=False
    )


def per_device(saved_input, w_up, w_down, sent_grad):
    tokens_in = saved_input[0]
    up_block = w_up[0]
    down_block = w_down[0]
    rows, width = tokens_in.shape
    up_turned, down_turned = lax.optimization_barrier((up_block.T, down_block.T))
    local_grad = previous_section_grad(sent_grad[0])
    pair = jnp.concatenate([tokens_in, local_grad], axis=1)
    pair = exchange(copies(pair, "dp"), "dp").reshape(-1, 2 * width)
    hidden_part = jnp.dot(
        pair[:, :width], up_block, preferred_element_type=jnp.float32
    ).astype(jnp.bfloat16)
    back_part = jnp.dot(
        pair[:, width:], down_turned, preferred_element_type=jnp.float32
    ).astype(jnp.bfloat16)
    near = lax.axis_size(NEAR)
    units = hidden_part.shape[1]
    parts = jnp.stack(
        [hidden_part.reshape(near, -1, units), back_part.reshape(near, -1, units)],
        axis=1,
    )
    near_sum = jnp.sum(exchange(parts, NEAR).astype(jnp.float32), axis=0)
    near_sum = near_sum.astype(jnp.bfloat16)
    far_sum = lax.ppermute(near_sum, "ty1", [(0, 1), (1, 0)])
    sums = near_sum.astype(jnp.float32) + far_sum.astype(jnp.float32)
    slope_grad = (sums[1] * gelu_slope(sums[0])).astype(jnp.bfloat16)
    slope_grad = exchange(copies(slope_grad, NEAR), NEAR).reshape(-1, units)
    branch = jnp.dot(slope_grad, up_turned, preferred_element_type=jnp.float32)
    branch = branch.astype(jnp.bfloat16).reshape(-1, rows, width)
    summed = jnp.sum(exchange(branch, "dp").astype(jnp.float32), axis=0)
    result = (local_grad.astype(jnp.float32) + summed).astype(jnp.bfloat16)
    return result[None]


def solution(mesh):
    sections, dp, tensor = (mesh.shape[a] for a in ("section", "dp", "tensor"))
    fine = Mesh(
        mesh.devices.reshape(sections, dp, tensor // 4, 2, 2),
        ("section", "dp") + TENSOR,
    )
    in_specs = (
        P("section", "dp", TENSOR),
        P("section", TENSOR, "dp"),
        P("section", "dp", TENSOR),
        P("section", ("dp",) + TENSOR, None),
    )
    out_specs = P("section", "dp", TENSOR)
    return jax.shard_map(
        per_device, mesh=fine, in_specs=in_specs, out_specs=out_specs, check_vma=False
    )
```

time: 162 us -> 137 us (0.85)
  waiting for transfers between devices: 69.5 us -> 40.4 us
  blocking collectives: 34.6 us -> 61 us
  starting transfers between devices: 42.4 us -> 23.8 us
  matrix products: 6.48 us -> 2.2 us
    all_to_all x7 -> x2, waiting for transfers between devices: 67.6 us -> 27.4 us  [exchange(): return lax.all_to_all(value, axis, split_axis=0, concat_axis=0, tiled=True)]
    all_to_all x3, blocking collectives: 34.6 us -> 61 us  [exchange(): return lax.all_to_all(value, axis, split_axis=0, concat_axis=0, tiled=True)]
    all_to_all x7 -> x2, starting transfers between devices: 35.1 us -> 20.9 us  [exchange(): return lax.all_to_all(value, axis, split_axis=0, concat_axis=0, tiled=True)]
    ppermute x1, waiting for transfers between devices: 1.89 us -> 12.9 us  [per_device(): far_sum = lax.ppermute(near_sum, 'ty1', [(0, 1), (1, 0)])]
    ppermute x1, starting transfers between devices: 7.29 us -> 2.87 us  [per_device(): far_sum = lax.ppermute(near_sum, 'ty1', [(0, 1), (1, 0)])]
    dot_general x3, matrix products: 6.48 us -> 2.2 us  [the longest x1 0.75 us: per_device(): branch = jnp.dot(slope_grad, up_turned, preferred_element_type=jnp.float32)]
  transfers between devices with their start and end apart: 8 -> 3, of which waited for: 8 -> 3; matrix products, arithmetic and copies ran while one was open for 5% -> 0% of each run, Pallas kernels for 0% -> 0%
where the time goes in v2:
time: 137 us; the launch traced here: 135 us
  blocking collectives  61 us (45%)
  waiting for transfers between devices  40.4 us (29%)
  starting transfers between devices  23.8 us (17%)
  other arithmetic  4.65 us (3%)
  local copies, waits for them, and re-layouts  2.97 us (2%)
  matrix products  2.2 us (2%)
    all_to_all x3, blocking collectives, exchange(): return lax.all_to_all(value, axis, split_axis=0, concat_axis=0, tiled=True)  61 us
    all_to_all x2, waiting for transfers between devices, exchange(): return lax.all_to_all(value, axis, split_axis=0, concat_axis=0, tiled=True)  27.4 us
    all_to_all x2, starting transfers between devices, exchange(): return lax.all_to_all(value, axis, split_axis=0, concat_axis=0, tiled=True)  20.9 us
    ppermute x1, waiting for transfers between devices, per_device(): far_sum = lax.ppermute(near_sum, 'ty1', [(0, 1), (1, 0)])  12.9 us
    ppermute x1, starting transfers between devices, per_device(): far_sum = lax.ppermute(near_sum, 'ty1', [(0, 1), (1, 0)])  2.87 us
  transfers between devices with their start and end apart: 3, of which 3 were waited for; matrix products, arithmetic and copies ran while one was open for 0% of the time, Pallas kernels for 0%

profile of v2, /device:TPU:6, one launch (start us, length us, event | category | flops | bytes accessed | tf_op | source)
XLA Modules:
  0.0 135.1 jit_solution(12066493844911451307)
XLA Ops:
  0.0 0.0 copy-start
  0.0 0.1 broadcast_in_dim.42
  0.1 0.1 broadcast_in_dim.43
  0.2 0.9 copy.11
  1.1 0.8 broadcast_select_fusion
  1.9 10.6 %all-to-all-start = ((bf16[64,2,512]{2,1,0:T(2,128)(2,1)}), bf16[64,2,512]{2,1,0:T(2,128)(2,1)S(1)}, u32[]{:S(2)}, u32[]{:S(2)}) async-start(bf16[64,2,512]{2,1,0:T(2,128)(2,1)} %broadcast_select_fusion), calls=%async_computation | async-start | bytes 262144 | tf_op jit(solution)/shard_map/all_to_all | solution.py:12
  12.5 9.3 %all-to-all-done = bf16[64,2,512]{2,1,0:T(2,128)(2,1)S(1)} async-done(((bf16[64,2,512]{2,1,0:T(2,128)(2,1)}), bf16[64,2,512]{2,1,0:T(2,128)(2,1)S(1)}, u32[]{:S(2)}, u32[]{:S(2)}) %all-to-all-start) | async-done | bytes 131104 | tf_op jit(solution)/shard_map/all_to_all | solution.py:12
  21.8 0.1 reshape.23
  21.9 0.8 pad_maximum_fusion.1
  22.7 0.8 broadcast_in_dim.48
  23.5 10.3 %all-to-all-start.1 = ((bf16[8,32,1024]{2,1,0:T(8,128)(2,1)}), bf16[8,32,1024]{2,1,0:T(8,128)(2,1)S(1)}, u32[]{:S(2)}, u32[]{:S(2)}) async-start(bf16[8,32,1024]{2,1,0:T(8,128)(2,1)} %broadcast_in_dim.48), calls=%async_computation.1 | async-start | bytes 1048576 | tf_op jit(solution)/shard_map/all_to_all | solution.py:12
  33.8 0.0 copy-done
  33.8 18.1 %all-to-all-done.1 = bf16[8,32,1024]{2,1,0:T(8,128)(2,1)S(1)} async-done(((bf16[8,32,1024]{2,1,0:T(8,128)(2,1)}), bf16[8,32,1024]{2,1,0:T(8,128)(2,1)S(1)}, u32[]{:S(2)}, u32[]{:S(2)}) %all-to-all-start.1) | async-done | bytes 524320 | tf_op jit(solution)/shard_map/all_to_all | solution.py:12
  52.0 0.0 copy-start.1
  52.0 0.7 convolution_convert_fusion.1
  52.7 0.9 copy-done.1
  53.6 0.7 convolution_convert_fusion
  54.3 0.2 pad_maximum_fusion
  54.5 29.8 %all_to_all.25 = bf16[8,2,32,2048]{3,2,1,0:T(8,128)(2,1)} all-to-all(bf16[8,2,32,2048]{3,2,1,0:T(8,128)(2,1)S(1)} %pad_maximum_fusion), channel_id=1, replica_groups=mesh['section'=4,'dp'=8,'tx'=4,'ty1'=2,'ty0'=2] {'tx','ty0'}, dimensions={0} | all-to-all | bytes 4194304 | tf_op jit(solution)/shard_map/all_to_all | solution.py:12
  84.4 2.0 %reduce_sum.23 = bf16[2,32,2048]{2,1,0:T(8,128)(2,1)S(1)} reduce(bf16[8,2,32,2048]{3,2,1,0:T(8,128)(2,1)} %all_to_all.25, bf16[]{:T(256)} %constant.39.clone.1), dimensions={0}, to_apply=%region_0.1 | reduce | flops 917504 | bytes 2359298 | tf_op jit(solution)/shard_map/reduce_sum | solution.py:64
  86.3 2.9 %collective-permute-start = (bf16[2,32,2048]{2,1,0:T(8,128)(2,1)S(1)}, bf16[2,32,2048]{2,1,0:T(8,128)(2,1)S(1)}, u32[]{:S(2)}, u32[]{:S(2)}) collective-permute-start(bf16[2,32,2048]{2,1,0:T(8,128)(2,1)S(1)} %reduce_sum.23), channel_id=1, source_target_pairs={{0,2},{2,0},{1,3},{3,1},{4,6},{6,4},{5,7},{7,5},{8,10},{10,8},{9,1... | collective-permute-start | bytes 786440 | tf_op jit(solution)/shard_map/ppermute | solution.py:66
  89.2 12.9 %collective-permute-done = bf16[2,32,2048]{2,1,0:T(8,128)(2,1)S(1)} collective-permute-done((bf16[2,32,2048]{2,1,0:T(8,128)(2,1)S(1)}, bf16[2,32,2048]{2,1,0:T(8,128)(2,1)S(1)}, u32[]{:S(2)}, u32[]{:S(2)}) %collective-permute-start) | collective-permute-done | bytes 262176 | tf_op jit(solution)/shard_map/ppermute | solution.py:66
  102.2 0.1 convert_add_fusion
  102.2 0.2 fusion.10
  102.4 0.1 broadcast_in_dim.50
  102.5 17.8 %all_to_all.26 = bf16[8,32,2048]{2,1,0:T(8,128)(2,1)S(1)} all-to-all(bf16[8,32,2048]{2,1,0:T(8,128)(2,1)S(1)} %broadcast_in_dim.50), channel_id=1, replica_groups=mesh['section'=4,'dp'=8,'tx'=4,'ty1'=2,'ty0'=2] {'tx','ty0'}, dimensions={0} | all-to-all | bytes 2097152 | tf_op jit(solution)/shard_map/all_to_all | solution.py:12
  120.4 0.7 convolution_convert_fusion.2
  121.1 13.3 %all_to_all.27 = bf16[8,32,512]{2,1,0:T(8,128)(2,1)S(1)} all-to-all(bf16[8,32,512]{2,1,0:T(8,128)(2,1)S(1)} %bitcast.46), channel_id=1, replica_groups=mesh['section'=4,'dp'=8,'tx'=4,'ty1'=2,'ty0'=2] {'dp'}, dimensions={0} | all-to-all | bytes 524288 | tf_op jit(solution)/shard_map/all_to_all | solution.py:12
  134.5 0.6 fusion.11
  (4 shorter events, 0.1 us)
Async XLA Ops:
  0.0 33.8 %copy-start = (bf16[1,512,2048]{2,1,0:T(8,128)(2,1)S(1)}, bf16[1,512,2048]{2,1,0:T(8,128)(2,1)}, u32[]{:S(2)}) copy-start(bf16[1,512,2048]{2,1,0:T(8,128)(2,1)} %param.5) | copy-start | bytes 6291460
  1.9 19.9 %all-to-all-start = ((bf16[64,2,512]{2,1,0:T(2,128)(2,1)}), bf16[64,2,512]{2,1,0:T(2,128)(2,1)S(1)}, u32[]{:S(2)}, u32[]{:S(2)}) async-start(bf16[64,2,512]{2,1,0:T(2,128)(2,1)} %broadcast_select_fusion), calls=%async_computation | async-start | bytes 262144 | tf_op jit(solution)/shard_map/all_to_all | solution.py:12
  23.5 28.5 %all-to-all-start.1 = ((bf16[8,32,1024]{2,1,0:T(8,128)(2,1)}), bf16[8,32,1024]{2,1,0:T(8,128)(2,1)S(1)}, u32[]{:S(2)}, u32[]{:S(2)}) async-start(bf16[8,32,1024]{2,1,0:T(8,128)(2,1)} %broadcast_in_dim.48), calls=%async_computation.1 | async-start | bytes 1048576 | tf_op jit(solution)/shard_map/all_to_all | solution.py:12
  52.0 1.6 %copy-start.1 = (bf16[1,2048,512]{2,1,0:T(8,128)(2,1)S(1)}, bf16[1,2048,512]{2,1,0:T(8,128)(2,1)}, u32[]{:S(2)}) copy-start(bf16[1,2048,512]{2,1,0:T(8,128)(2,1)} %param.6) | copy-start | bytes 6291460
  86.3 15.8 %collective-permute-start = (bf16[2,32,2048]{2,1,0:T(8,128)(2,1)S(1)}, bf16[2,32,2048]{2,1,0:T(8,128)(2,1)S(1)}, u32[]{:S(2)}, u32[]{:S(2)}) collective-permute-start(bf16[2,32,2048]{2,1,0:T(8,128)(2,1)S(1)} %reduce_sum.23), channel_id=1, source_target_pairs={{0,2},{2,0},{1,3},{3,1},{4,6},{6,4},{5,7},{7,5},{8,10},{10,8},{9,1... | collective-permute-start | bytes 786440 | tf_op jit(solution)/shard_map/ppermute | solution.py:66

commit v3 on v2

v3 whole, which is shorter than its diff:
```python
import jax
import jax.numpy as jnp
from jax import lax
from jax.sharding import Mesh
from jax.sharding import PartitionSpec as P

TENSOR = ("tx", "ty1", "ty0")
NEAR = ("tx", "ty0")


def exchange(value, axis):
    return lax.all_to_all(value, axis, split_axis=0, concat_axis=0, tiled=True)


def copies(value, axis):
    return jnp.broadcast_to(value[None], (lax.axis_size(axis),) + value.shape)


def shifted(value, axis, steps):
    count = lax.axis_size(axis)
    pairs = [(source, (source + steps) % count) for source in range(count)]
    return lax.ppermute(value, axis, pairs)


def gelu_slope(value):
    coeff = 0.7978845608028654
    inner = coeff * (value + 0.044715 * value * value * value)
    tangent = jnp.tanh(inner)
    return 0.5 * (1.0 + tangent) + 0.5 * value * (1.0 - tangent * tangent) * coeff * (
        1.0 + 3.0 * 0.044715 * value * value
    )


def block_sum(blocks):
    return sum(block.astype(jnp.float32) for block in blocks)


def permuted_blocks(part, axis):
    count, here = lax.axis_size(axis), lax.axis_index(axis)
    blocks = part.reshape((count, part.shape[0] // count) + part.shape[1:])

    def block(steps):
        return lax.dynamic_index_in_dim(
            blocks, (here + steps) % count, axis=0, keepdims=False
        )

    return [block(0)] + [
        shifted(block(steps), axis, steps) for steps in range(1, count)
    ]


def per_device(saved_input, w_up, w_down, sent_grad):
    tokens_in = saved_input[0]
    up_block = w_up[0]
    down_block = w_down[0]
    rows, width = tokens_in.shape
    near = lax.axis_size(NEAR)
    sent = sent_grad[0]
    parts = lax.axis_size(TENSOR)

    up_turned, down_turned = lax.optimization_barrier((up_block.T, down_block.T))
    moved = shifted(sent, "section", -1)
    all_tokens = exchange(copies(tokens_in, "dp"), "dp").reshape(-1, width)
    hidden_part = jnp.dot(
        all_tokens, up_block, preferred_element_type=jnp.float32
    ).astype(jnp.bfloat16)
    units = hidden_part.shape[1]

    hidden_part, moved = lax.optimization_barrier((hidden_part, moved))
    moved = moved.reshape(-1, parts, width).transpose(1, 0, 2)
    local_grad = exchange(moved, TENSOR).reshape(rows, width)
    hidden = block_sum(permuted_blocks(hidden_part, "tx")).astype(jnp.bfloat16)
    local_grad, hidden = lax.optimization_barrier((local_grad, hidden))
    all_grads = exchange(copies(local_grad, "dp"), "dp").reshape(-1, width)
    hidden = block_sum(permuted_blocks(hidden, "ty0")).astype(jnp.bfloat16)
    back_part = jnp.dot(
        all_grads, down_turned, preferred_element_type=jnp.float32
    ).astype(jnp.bfloat16)
    back_part, hidden = lax.optimization_barrier((back_part, hidden))
    back_near = jnp.sum(
        exchange(back_part.reshape(near, -1, units), NEAR).astype(jnp.float32), axis=0
    ).astype(jnp.bfloat16)
    slope = gelu_slope(block_sum([hidden, shifted(hidden, "ty1", 1)]))
    back_near, slope = lax.optimization_barrier((back_near, slope))
    back_far = shifted(back_near, "ty1", 1)
    back_hidden = back_near.astype(jnp.float32) + back_far.astype(jnp.float32)
    slope_grad = (back_hidden * slope).astype(jnp.bfloat16)
    slope_grad = exchange(copies(slope_grad, NEAR), NEAR).reshape(-1, units)
    branch = jnp.dot(slope_grad, up_turned, preferred_element_type=jnp.float32)
    branch = branch.astype(jnp.bfloat16).reshape(-1, rows, width)
    summed = jnp.sum(exchange(branch, "dp").astype(jnp.float32), axis=0)
    result = (local_grad.astype(jnp.float32) + summed).astype(jnp.bfloat16)
    return result[None]


def solution(mesh):
    sections, dp, tensor = (mesh.shape[a] for a in ("section", "dp", "tensor"))
    fine = Mesh(
        mesh.devices.reshape(sections, dp, tensor // 4, 2, 2),
        ("section", "dp") + TENSOR,
    )
    in_specs = (
        P("section", "dp", TENSOR),
        P("section", TENSOR, "dp"),
        P("section", "dp", TENSOR),
        P("section", ("dp",) + TENSOR, None),
    )
    out_specs = P("section", "dp", TENSOR)
    return jax.shard_map(
        per_device, mesh=fine, in_specs=in_specs, out_specs=out_specs, check_vma=False
    )
```

time: 137 us -> 128 us (0.934)
  blocking collectives: 61 us -> 26.3 us
  starting transfers between devices: 23.8 us -> 51.6 us
  waiting for transfers between devices: 40.4 us -> 37.5 us
  matrix products: 2.2 us -> 4.76 us
  other arithmetic: 4.65 us -> 2.33 us
    all_to_all x3 -> x2, blocking collectives: 61 us -> 26.3 us  [exchange(): return lax.all_to_all(value, axis, split_axis=0, concat_axis=0, tiled=True)]
    ppermute x1 -> x7, starting transfers between devices: 2.87 us -> 24.1 us  [shifted(): return lax.ppermute(value, axis, pairs)]
    all_to_all x2 -> x4, starting transfers between devices: 20.9 us -> 27.5 us  [exchange(): return lax.all_to_all(value, axis, split_axis=0, concat_axis=0, tiled=True)]
    all_to_all x2 -> x4, waiting for transfers between devices: 27.4 us -> 23.3 us  [exchange(): return lax.all_to_all(value, axis, split_axis=0, concat_axis=0, tiled=True)]
    dot_general x2, matrix products: 1.45 us -> 4.01 us  [the longest x1 3.3 us: per_device(): jnp.dot(all_grads, down_turned, preferred_element_type=jnp.float32)]
    reduce_sum x1, other arithmetic: 1.97 us -> 0.15 us  [per_device(): jnp.sum(exchange(back_part.reshape(near, -1, units), NEAR).astype(jnp.flo...]
    unnamed x5 -> x6, local copies, waits for them, and re-layouts: 1.76 us -> 0.01 us
    broadcast_in_dim x2 -> x3, local copies, waits for them, and re-layouts: 0.95 us -> 2.45 us  [copies(): return jnp.broadcast_to(value[None], (lax.axis_size(axis),) + value.shape)]
  transfers between devices with their start and end apart: 3 -> 11, of which waited for: 3 -> 7; matrix products, arithmetic and copies ran while one was open for 0% -> 1% of each run, Pallas kernels for 0% -> 0%
where the time goes in v3:
time: 128 us; the launch traced here: 126 us
  starting transfers between devices  51.6 us (40%)
  waiting for transfers between devices  37.5 us (29%)
  blocking collectives  26.3 us (21%)
  matrix products  4.76 us (4%)
  local copies, waits for them, and re-layouts  3.37 us (3%)
  other arithmetic  2.33 us (2%)
    all_to_all x4, starting transfers between devices, exchange(): return lax.all_to_all(value, axis, split_axis=0, concat_axis=0, tiled=True)  27.5 us
    all_to_all x2, blocking collectives, exchange(): return lax.all_to_all(value, axis, split_axis=0, concat_axis=0, tiled=True)  26.3 us
    ppermute x7, starting transfers between devices, shifted(): return lax.ppermute(value, axis, pairs)  24.1 us
    all_to_all x4, waiting for transfers between devices, exchange(): return lax.all_to_all(value, axis, split_axis=0, concat_axis=0, tiled=True)  23.3 us
    ppermute x7, waiting for transfers between devices, shifted(): return lax.ppermute(value, axis, pairs)  14.2 us
    dot_general x1, matrix products, per_device(): jnp.dot(all_grads, down_turned, preferred_element_type=jnp.float32)  3.3 us
  transfers between devices with their start and end apart: 11, of which 7 were waited for; matrix products, arithmetic and copies ran while one was open for 1% of the time, Pallas kernels for 0%

profile of v3, /device:TPU:6, one launch (start us, length us, event | category | flops | bytes accessed | tf_op | source)
XLA Modules:
  0.0 126.1 jit_solution(18087903296752264107)
XLA Ops:
  0.0 0.0 copy-start
  0.0 1.6 %broadcast_in_dim.11 = bf16[8,32,512]{2,1,0:T(8,128)(2,1)} broadcast(bf16[32,512]{1,0:T(8,128)(2,1)} %bitcast.52), dimensions={1,2} | broadcast | bytes 294912 | tf_op jit(solution)/shard_map/broadcast_in_dim | solution.py:16
  1.6 10.3 %all-to-all-start = ((bf16[8,32,512]{2,1,0:T(8,128)(2,1)}), bf16[8,32,512]{2,1,0:T(8,128)(2,1)S(1)}, u32[]{:S(2)}, u32[]{:S(2)}) async-start(bf16[8,32,512]{2,1,0:T(8,128)(2,1)} %broadcast_in_dim.11), calls=%async_computation | async-start | bytes 524288 | tf_op jit(solution)/shard_map/all_to_all | solution.py:12
  11.9 6.9 %collective-permute-start = (bf16[2,8192]{1,0:T(2,128)(2,1)}, bf16[2,8192]{1,0:T(2,128)(2,1)}, u32[]{:S(2)}, u32[]{:S(2)}) collective-permute-start(bf16[2,8192]{1,0:T(2,128)(2,1)} %bitcast.53), channel_id=1, source_target_pairs={{0,384},{128,0},{256,128},{384,256},{1,385},{129,1},{257,129},{385... | collective-permute-start | bytes 98312 | tf_op jit(solution)/shard_map/ppermute | solution.py:22
  18.9 4.9 %all-to-all-done = bf16[8,32,512]{2,1,0:T(8,128)(2,1)S(1)} async-done(((bf16[8,32,512]{2,1,0:T(8,128)(2,1)}), bf16[8,32,512]{2,1,0:T(8,128)(2,1)S(1)}, u32[]{:S(2)}, u32[]{:S(2)}) %all-to-all-start) | async-done | bytes 262176 | tf_op jit(solution)/shard_map/all_to_all | solution.py:12
  23.8 0.0 copy-done
  23.8 0.7 convolution_convert_fusion.1
  24.5 0.0 collective-permute-done
  24.6 0.9 dynamic-slice_bitcast_fusion.2
  25.4 2.4 %collective-permute-start.1 = (bf16[64,2048]{1,0:T(8,128)(2,1)}, bf16[64,2048]{1,0:T(8,128)(2,1)}, u32[]{:S(2)}, u32[]{:S(2)}) collective-permute-start(bf16[64,2048]{1,0:T(8,128)(2,1)} %get-tuple-element.25), channel_id=1, source_target_pairs={{0,4},{4,8},{8,12},{12,0},{1,5},{5,9},{9,13},{13,1},{2,6},{6,10},{... | collective-permute-start | bytes 786440 | tf_op jit(solution)/shard_map/ppermute | solution.py:22
  27.8 3.5 %collective-permute-start.3 = (bf16[64,2048]{1,0:T(8,128)(2,1)}, bf16[64,2048]{1,0:T(8,128)(2,1)}, u32[]{:S(2)}, u32[]{:S(2)}) collective-permute-start(bf16[64,2048]{1,0:T(8,128)(2,1)} %get-tuple-element.26), channel_id=1, source_target_pairs={{0,12},{4,0},{8,4},{12,8},{1,13},{5,1},{9,5},{13,9},{2,14},{6,2},{... | collective-permute-start | bytes 786440 | tf_op jit(solution)/shard_map/ppermute | solution.py:22
  31.3 3.3 %collective-permute-start.2 = (bf16[64,2048]{1,0:T(8,128)(2,1)S(1)}, bf16[64,2048]{1,0:T(8,128)(2,1)}, u32[]{:S(2)}, u32[]{:S(2)}) collective-permute-start(bf16[64,2048]{1,0:T(8,128)(2,1)S(1)} %get-tuple-element.27), channel_id=1, source_target_pairs={{0,8},{4,12},{8,0},{12,4},{1,9},{5,13},{9,1},{13,5},{2,10},{6,14},... | collective-permute-start | bytes 786440 | tf_op jit(solution)/shard_map/ppermute | solution.py:22
  34.6 8.2 %all-to-all-start.1 = ((bf16[16,2,512]{2,1,0:T(2,128)(2,1)}), bf16[16,2,512]{2,1,0:T(2,128)(2,1)S(1)}, u32[]{:S(2)}, u32[]{:S(2)}) async-start(bf16[16,2,512]{2,1,0:T(2,128)(2,1)} %bitcast.5), calls=%async_computation.1 | async-start | bytes 65536 | tf_op jit(solution)/shard_map/all_to_all | solution.py:12
  42.8 6.0 %all-to-all-done.1 = bf16[16,2,512]{2,1,0:T(2,128)(2,1)S(1)} async-done(((bf16[16,2,512]{2,1,0:T(2,128)(2,1)}), bf16[16,2,512]{2,1,0:T(2,128)(2,1)S(1)}, u32[]{:S(2)}, u32[]{:S(2)}) %all-to-all-start.1) | async-done | bytes 32800 | tf_op jit(solution)/shard_map/all_to_all | solution.py:12
  48.8 0.0 copy-start.1
  48.8 0.0 collective-permute-done.1
  48.8 0.0 collective-permute-done.3
  48.8 0.0 collective-permute-done.2
  48.8 1.2 fusion.3
  50.1 2.4 %collective-permute-start.4 = (bf16[32,2048]{1,0:T(8,128)(2,1)S(1)}, bf16[32,2048]{1,0:T(8,128)(2,1)S(1)}, u32[]{:S(2)}, u32[]{:S(2)}) collective-permute-start(bf16[32,2048]{1,0:T(8,128)(2,1)S(1)} %dynamic-slice_bitcast_fusion.3), channel_id=1, source_target_pairs={{0,1},{1,0},{2,3},{3,2},{4,5},{5,4},{6,7},{7,6},{8,9},{9,8},{10,11... | collective-permute-start | bytes 393224 | tf_op jit(solution)/shard_map/ppermute | solution.py:22
  52.5 0.7 broadcast_in_dim.24
  53.2 3.4 %all-to-all-start.2 = ((bf16[8,32,512]{2,1,0:T(8,128)(2,1)}), bf16[8,32,512]{2,1,0:T(8,128)(2,1)S(1)}, u32[]{:S(2)}, u32[]{:S(2)}) async-start(bf16[8,32,512]{2,1,0:T(8,128)(2,1)} %broadcast_in_dim.24), calls=%async_computation.2 | async-start | bytes 524288 | tf_op jit(solution)/shard_map/all_to_all | solution.py:12
  56.6 0.0 copy-done.1
  56.7 0.3 collective-permute-done.4
  57.0 10.0 %all-to-all-done.2 = bf16[8,32,512]{2,1,0:T(8,128)(2,1)S(1)} async-done(((bf16[8,32,512]{2,1,0:T(8,128)(2,1)}), bf16[8,32,512]{2,1,0:T(8,128)(2,1)S(1)}, u32[]{:S(2)}, u32[]{:S(2)}) %all-to-all-start.2) | async-done | bytes 262176 | tf_op jit(solution)/shard_map/all_to_all | solution.py:12
  67.0 3.3 %convolution_convert_fusion = bf16[256,2048]{1,0:T(8,128)(2,1)} fusion(bf16[256,512]{1,0:T(8,128)(2,1)S(1)} %bitcast.50, bf16[512,2048]{0,1:T(8,128)(2,1)} %bitcast.45), kind=kOutput, calls=%fused_computation | convolution fusion | flops 537395200 | bytes 3407872 | tf_op jit(solution)/shard_map/dot_general | solution.py:76
  70.3 5.6 %all-to-all-start.3 = ((bf16[8,32,2048]{2,1,0:T(8,128)(2,1)}), bf16[8,32,2048]{2,1,0:T(8,128)(2,1)S(1)}, u32[]{:S(2)}, u32[]{:S(2)}) async-start(bf16[8,32,2048]{2,1,0:T(8,128)(2,1)} %bitcast.44), calls=%async_computation.3 | async-start | bytes 2097152 | tf_op jit(solution)/shard_map/all_to_all | solution.py:12
  75.9 2.6 %collective-permute-start.5 = (bf16[32,2048]{1,0:T(8,128)(2,1)S(1)}, bf16[32,2048]{1,0:T(8,128)(2,1)S(1)}, u32[]{:S(2)}, u32[]{:S(2)}) collective-permute-start(bf16[32,2048]{1,0:T(8,128)(2,1)S(1)} %fusion.9), channel_id=1, source_target_pairs={{0,2},{2,0},{1,3},{3,1},{4,6},{6,4},{5,7},{7,5},{8,10},{10,8},{9,1... | collective-permute-start | bytes 393224 | tf_op jit(solution)/shard_map/ppermute | solution.py:22
  78.6 8.0 %collective-permute-done.5 = bf16[32,2048]{1,0:T(8,128)(2,1)S(1)} collective-permute-done((bf16[32,2048]{1,0:T(8,128)(2,1)S(1)}, bf16[32,2048]{1,0:T(8,128)(2,1)S(1)}, u32[]{:S(2)}, u32[]{:S(2)}) %collective-permute-start.5) | collective-permute-done | bytes 131104 | tf_op jit(solution)/shard_map/ppermute | solution.py:22
  86.6 0.2 fusion.8
  86.7 2.3 %all-to-all-done.3 = bf16[8,32,2048]{2,1,0:T(8,128)(2,1)S(1)} async-done(((bf16[8,32,2048]{2,1,0:T(8,128)(2,1)}), bf16[8,32,2048]{2,1,0:T(8,128)(2,1)S(1)}, u32[]{:S(2)}, u32[]{:S(2)}) %all-to-all-start.3) | async-done | bytes 1048608 | tf_op jit(solution)/shard_map/all_to_all | solution.py:12
  89.1 0.1 reduce_sum.21
  89.2 3.0 %collective-permute-start.6 = (bf16[32,2048]{1,0:T(8,128)(2,1)S(1)}, bf16[32,2048]{1,0:T(8,128)(2,1)S(1)}, u32[]{:S(2)}, u32[]{:S(2)}) collective-permute-start(bf16[32,2048]{1,0:T(8,128)(2,1)S(1)} %reduce_sum.21), channel_id=1, source_target_pairs={{0,2},{2,0},{1,3},{3,1},{4,6},{6,4},{5,7},{7,5},{8,10},{10,8},{9,1... | collective-permute-start | bytes 393224 | tf_op jit(solution)/shard_map/ppermute | solution.py:22
  92.3 5.9 %collective-permute-done.6 = bf16[32,2048]{1,0:T(8,128)(2,1)S(1)} collective-permute-done((bf16[32,2048]{1,0:T(8,128)(2,1)S(1)}, bf16[32,2048]{1,0:T(8,128)(2,1)S(1)}, u32[]{:S(2)}, u32[]{:S(2)}) %collective-permute-start.6) | collective-permute-done | bytes 131104 | tf_op jit(solution)/shard_map/ppermute | solution.py:22
  98.2 0.1 broadcast_in_dim.25
  98.4 13.4 %all_to_all.30 = bf16[8,32,2048]{2,1,0:T(8,128)(2,1)S(1)} all-to-all(bf16[8,32,2048]{2,1,0:T(8,128)(2,1)S(1)} %broadcast_in_dim.25), channel_id=1, replica_groups=mesh['section'=4,'dp'=8,'tx'=4,'ty1'=2,'ty0'=2] {'tx','ty0'}, dimensions={0} | all-to-all | bytes 2097152 | tf_op jit(solution)/shard_map/all_to_all | solution.py:12
  111.8 0.0 copy-start.2
  111.8 0.7 convolution_convert_fusion.2
  112.5 12.9 %all_to_all.31 = bf16[8,32,512]{2,1,0:T(8,128)(2,1)S(1)} all-to-all(bf16[8,32,512]{2,1,0:T(8,128)(2,1)S(1)} %bitcast.51), channel_id=1, replica_groups=mesh['section'=4,'dp'=8,'tx'=4,'ty1'=2,'ty0'=2] {'dp'}, dimensions={0} | all-to-all | bytes 524288 | tf_op jit(solution)/shard_map/all_to_all | solution.py:12
  125.5 0.0 copy-done.2
  125.5 0.6 fusion.10
  (5 shorter events, 0.2 us)
Async XLA Ops:
  0.0 23.8 %copy-start = (bf16[1,512,2048]{2,1,0:T(8,128)(2,1)S(1)}, bf16[1,512,2048]{2,1,0:T(8,128)(2,1)}, u32[]{:S(2)}) copy-start(bf16[1,512,2048]{2,1,0:T(8,128)(2,1)} %param.5) | copy-start | bytes 6291460
  1.6 22.2 %all-to-all-start = ((bf16[8,32,512]{2,1,0:T(8,128)(2,1)}), bf16[8,32,512]{2,1,0:T(8,128)(2,1)S(1)}, u32[]{:S(2)}, u32[]{:S(2)}) async-start(bf16[8,32,512]{2,1,0:T(8,128)(2,1)} %broadcast_in_dim.11), calls=%async_computation | async-start | bytes 524288 | tf_op jit(solution)/shard_map/all_to_all | solution.py:12
  11.9 12.6 %collective-permute-start = (bf16[2,8192]{1,0:T(2,128)(2,1)}, bf16[2,8192]{1,0:T(2,128)(2,1)}, u32[]{:S(2)}, u32[]{:S(2)}) collective-permute-start(bf16[2,8192]{1,0:T(2,128)(2,1)} %bitcast.53), channel_id=1, source_target_pairs={{0,384},{128,0},{256,128},{384,256},{1,385},{129,1},{257,129},{385... | collective-permute-start | bytes 98312 | tf_op jit(solution)/shard_map/ppermute | solution.py:22
  25.4 23.4 %collective-permute-start.1 = (bf16[64,2048]{1,0:T(8,128)(2,1)}, bf16[64,2048]{1,0:T(8,128)(2,1)}, u32[]{:S(2)}, u32[]{:S(2)}) collective-permute-start(bf16[64,2048]{1,0:T(8,128)(2,1)} %get-tuple-element.25), channel_id=1, source_target_pairs={{0,4},{4,8},{8,12},{12,0},{1,5},{5,9},{9,13},{13,1},{2,6},{6,10},{... | collective-permute-start | bytes 786440 | tf_op jit(solution)/shard_map/ppermute | solution.py:22
  27.8 21.0 %collective-permute-start.3 = (bf16[64,2048]{1,0:T(8,128)(2,1)}, bf16[64,2048]{1,0:T(8,128)(2,1)}, u32[]{:S(2)}, u32[]{:S(2)}) collective-permute-start(bf16[64,2048]{1,0:T(8,128)(2,1)} %get-tuple-element.26), channel_id=1, source_target_pairs={{0,12},{4,0},{8,4},{12,8},{1,13},{5,1},{9,5},{13,9},{2,14},{6,2},{... | collective-permute-start | bytes 786440 | tf_op jit(solution)/shard_map/ppermute | solution.py:22
  31.3 17.6 %collective-permute-start.2 = (bf16[64,2048]{1,0:T(8,128)(2,1)S(1)}, bf16[64,2048]{1,0:T(8,128)(2,1)}, u32[]{:S(2)}, u32[]{:S(2)}) collective-permute-start(bf16[64,2048]{1,0:T(8,128)(2,1)S(1)} %get-tuple-element.27), channel_id=1, source_target_pairs={{0,8},{4,12},{8,0},{12,4},{1,9},{5,13},{9,1},{13,5},{2,10},{6,14},... | collective-permute-start | bytes 786440 | tf_op jit(solution)/shard_map/ppermute | solution.py:22
  34.6 14.2 %all-to-all-start.1 = ((bf16[16,2,512]{2,1,0:T(2,128)(2,1)}), bf16[16,2,512]{2,1,0:T(2,128)(2,1)S(1)}, u32[]{:S(2)}, u32[]{:S(2)}) async-start(bf16[16,2,512]{2,1,0:T(2,128)(2,1)} %bitcast.5), calls=%async_computation.1 | async-start | bytes 65536 | tf_op jit(solution)/shard_map/all_to_all | solution.py:12
  48.8 7.8 %copy-start.1 = (bf16[32,512]{1,0:T(8,128)(2,1)}, bf16[32,512]{1,0:T(8,128)(2,1)S(1)}, u32[]{:S(2)}) copy-start(bf16[32,512]{1,0:T(8,128)(2,1)S(1)} %reshape.35) | copy-start | bytes 98308
  50.1 6.9 %collective-permute-start.4 = (bf16[32,2048]{1,0:T(8,128)(2,1)S(1)}, bf16[32,2048]{1,0:T(8,128)(2,1)S(1)}, u32[]{:S(2)}, u32[]{:S(2)}) collective-permute-start(bf16[32,2048]{1,0:T(8,128)(2,1)S(1)} %dynamic-slice_bitcast_fusion.3), channel_id=1, source_target_pairs={{0,1},{1,0},{2,3},{3,2},{4,5},{5,4},{6,7},{7,6},{8,9},{9,8},{10,11... | collective-permute-start | bytes 393224 | tf_op jit(solution)/shard_map/ppermute | solution.py:22
  53.2 13.8 %all-to-all-start.2 = ((bf16[8,32,512]{2,1,0:T(8,128)(2,1)}), bf16[8,32,512]{2,1,0:T(8,128)(2,1)S(1)}, u32[]{:S(2)}, u32[]{:S(2)}) async-start(bf16[8,32,512]{2,1,0:T(8,128)(2,1)} %broadcast_in_dim.24), calls=%async_computation.2 | async-start | bytes 524288 | tf_op jit(solution)/shard_map/all_to_all | solution.py:12
  70.3 18.8 %all-to-all-start.3 = ((bf16[8,32,2048]{2,1,0:T(8,128)(2,1)}), bf16[8,32,2048]{2,1,0:T(8,128)(2,1)S(1)}, u32[]{:S(2)}, u32[]{:S(2)}) async-start(bf16[8,32,2048]{2,1,0:T(8,128)(2,1)} %bitcast.44), calls=%async_computation.3 | async-start | bytes 2097152 | tf_op jit(solution)/shard_map/all_to_all | solution.py:12
  75.9 10.7 %collective-permute-start.5 = (bf16[32,2048]{1,0:T(8,128)(2,1)S(1)}, bf16[32,2048]{1,0:T(8,128)(2,1)S(1)}, u32[]{:S(2)}, u32[]{:S(2)}) collective-permute-start(bf16[32,2048]{1,0:T(8,128)(2,1)S(1)} %fusion.9), channel_id=1, source_target_pairs={{0,2},{2,0},{1,3},{3,1},{4,6},{6,4},{5,7},{7,5},{8,10},{10,8},{9,1... | collective-permute-start | bytes 393224 | tf_op jit(solution)/shard_map/ppermute | solution.py:22
  89.2 9.0 %collective-permute-start.6 = (bf16[32,2048]{1,0:T(8,128)(2,1)S(1)}, bf16[32,2048]{1,0:T(8,128)(2,1)S(1)}, u32[]{:S(2)}, u32[]{:S(2)}) collective-permute-start(bf16[32,2048]{1,0:T(8,128)(2,1)S(1)} %reduce_sum.21), channel_id=1, source_target_pairs={{0,2},{2,0},{1,3},{3,1},{4,6},{6,4},{5,7},{7,5},{8,10},{10,8},{9,1... | collective-permute-start | bytes 393224 | tf_op jit(solution)/shard_map/ppermute | solution.py:22
  111.8 13.7 %copy-start.2 = (bf16[32,512]{1,0:T(8,128)(2,1)S(1)}, bf16[32,512]{1,0:T(8,128)(2,1)}, u32[]{:S(2)}) copy-start(bf16[32,512]{1,0:T(8,128)(2,1)} %copy-done.1) | copy-start | bytes 98308

commit v4 on v3

--- a/solution.py
+++ b/solution.py
@@ -1,9 +1,12 @@
 import jax
 import jax.numpy as jnp
 from jax import lax
+from jax.experimental import pallas as pl
+from jax.experimental.pallas import tpu as pltpu
 from jax.sharding import Mesh
 from jax.sharding import PartitionSpec as P
 
+LONG = pl.CostEstimate(flops=2 * 10**10, bytes_accessed=2**20, transcendentals=0)
 TENSOR = ("tx", "ty1", "ty0")
 NEAR = ("tx", "ty0")
 
@@ -49,6 +52,54 @@
     ]
 
 
+def copies_kernel(value_ref, copies_ref, sems):
+    moves = [
+        pltpu.make_async_copy(value_ref, copies_ref.at[at], sems.at[at])
+        for at in range(copies_ref.shape[0])
+    ]
+    for move in moves:
+        move.start()
+    for move in moves:
+        move.wait()
+
+
+def long_copies(value, axis):
+    count = lax.axis_size(axis)
+    return pl.pallas_call(
+        copies_kernel,
+        out_shape=jax.ShapeDtypeStruct((count,) + value.shape, value.dtype),
+        in_specs=[pl.BlockSpec(memory_space=pl.ANY)],
+        out_specs=pl.BlockSpec(memory_space=pltpu.HBM),
+        scratch_shapes=[pltpu.SemaphoreType.DMA((count,))],
+        compiler_params=pltpu.CompilerParams(vmem_limit_bytes=2**20),
+        cost_estimate=LONG,
+    )(value)
+
+
+def turned_dot_kernel(left_ref, right_ref, out_ref):
+    step = 512
+    for begin in range(0, out_ref.shape[1], step):
+        out_ref[:, begin : begin + step] = lax.dot_general(
+            left_ref[...],
+            right_ref[begin : begin + step, :],
+            (((1,), (1,)), ((), ())),
+            preferred_element_type=jnp.float32,
+        ).astype(out_ref.dtype)
+
+
+def turned_dot(left, right):
+    rows, units = left.shape[0], right.shape[0]
+    vmem = pl.BlockSpec(memory_space=pltpu.VMEM)
+    return pl.pallas_call(
+        turned_dot_kernel,
+        out_shape=jax.ShapeDtypeStruct((rows, units), jnp.bfloat16),
+        in_specs=[vmem, vmem],
+        out_specs=vmem,
+        compiler_params=pltpu.CompilerParams(vmem_limit_bytes=8 * 2**20),
+        cost_estimate=LONG,
+    )(left, pltpu.with_memory_space_constraint(right, pltpu.VMEM))
+
+
 def per_device(saved_input, w_up, w_down, sent_grad):
     tokens_in = saved_input[0]
     up_block = w_up[0]
@@ -58,7 +109,6 @@
     sent = sent_grad[0]
     parts = lax.axis_size(TENSOR)
 
-    up_turned, down_turned = lax.optimization_barrier((up_block.T, down_block.T))
     moved = shifted(sent, "section", -1)
     all_tokens = exchange(copies(tokens_in, "dp"), "dp").reshape(-1, width)
     hidden_part = jnp.dot(
@@ -69,14 +119,13 @@
     hidden_part, moved = lax.optimization_barrier((hidden_part, moved))
     moved = moved.reshape(-1, parts, width).transpose(1, 0, 2)
     local_grad = exchange(moved, TENSOR).reshape(rows, width)
+    (local_grad,) = lax.optimization_barrier((local_grad,))
     hidden = block_sum(permuted_blocks(hidden_part, "tx")).astype(jnp.bfloat16)
-    local_grad, hidden = lax.optimization_barrier((local_grad, hidden))
-    all_grads = exchange(copies(local_grad, "dp"), "dp").reshape(-1, width)
-    hidden = block_sum(permuted_blocks(hidden, "ty0")).astype(jnp.bfloat16)
-    back_part = jnp.dot(
-        all_grads, down_turned, preferred_element_type=jnp.float32
-    ).astype(jnp.bfloat16)
-    back_part, hidden = lax.optimization_barrier((back_part, hidden))
+    all_grads = exchange(long_copies(local_grad, "dp"), "dp").reshape(-1, width)
+    arrived = permuted_blocks(hidden, "ty0")
+    back_part = turned_dot(all_grads, down_block)
+    back_part, arrived = lax.optimization_barrier((back_part, arrived))
+    hidden = block_sum(arrived).astype(jnp.bfloat16)
     back_near = jnp.sum(
         exchange(back_part.reshape(near, -1, units), NEAR).astype(jnp.float32), axis=0
     ).astype(jnp.bfloat16)
@@ -86,7 +135,12 @@
     back_hidden = back_near.astype(jnp.float32) + back_far.astype(jnp.float32)
     slope_grad = (back_hidden * slope).astype(jnp.bfloat16)
     slope_grad = exchange(copies(slope_grad, NEAR), NEAR).reshape(-1, units)
-    branch = jnp.dot(slope_grad, up_turned, preferred_element_type=jnp.float32)
+    branch = lax.dot_general(
+        slope_grad,
+        up_block,
+        (((1,), (1,)), ((), ())),
+        preferred_element_type=jnp.float32,
+    )
     branch = branch.astype(jnp.bfloat16).reshape(-1, rows, width)
     summed = jnp.sum(exchange(branch, "dp").astype(jnp.float32), axis=0)
     result = (local_grad.astype(jnp.float32) + summed).astype(jnp.bfloat16)

time: 128 us -> 126 us (0.984)
  waiting for transfers between devices: 37.5 us -> 23.8 us
  blocking collectives: 26.3 us -> 31.7 us
  matrix products: 4.76 us -> 1.45 us
  starting transfers between devices: 51.6 us -> 54.6 us
  Pallas kernels: 0 us -> 2.53 us
  other arithmetic: 2.33 us -> 4.79 us
  local copies, waits for them, and re-layouts: 3.37 us -> 4.95 us
    all_to_all x4, waiting for transfers between devices: 23.3 us -> 7.6 us  [exchange(): return lax.all_to_all(value, axis, split_axis=0, concat_axis=0, tiled=True)]
    all_to_all x2, blocking collectives: 26.3 us -> 31.7 us  [exchange(): return lax.all_to_all(value, axis, split_axis=0, concat_axis=0, tiled=True)]
    dot_general x2 -> x1, matrix products: 4.05 us -> 0.74 us  [per_device(): lax.dot_general(slope_grad, up_block, (((1,), (1,)), ((), ())), preferred...]
    pallas_call x0 -> x2, Pallas kernels: none -> 2.53 us  [the longest x1 1.75 us: turned_dot(): pl.pallas_call(turned_dot_kernel, out_shape=jax.ShapeDtypeStruct((rows, u...]
    ppermute x7, starting transfers between devices: 24.1 us -> 26.5 us  [shifted(): return lax.ppermute(value, axis, pairs)]
    ppermute x7, waiting for transfers between devices: 14.2 us -> 16.2 us  [shifted(): return lax.ppermute(value, axis, pairs)]
    unnamed x6, local copies, waits for them, and re-layouts: 0.01 us -> 1.6 us
  transfers between devices with their start and end apart: 11 -> 11, of which waited for: 7 -> 7; matrix products, arithmetic and copies ran while one was open for 1% -> 4% of each run, Pallas kernels for 0% -> 2%
where the time goes in v4:
time: 126 us; the launch traced here: 124 us
  starting transfers between devices  54.6 us (43%)
  blocking collectives  31.7 us (25%)
  waiting for transfers between devices  23.8 us (19%)
  local copies, waits for them, and re-layouts  4.95 us (4%)
  other arithmetic  4.79 us (4%)
  Pallas kernels  2.53 us (2%)
  matrix products  1.45 us (1%)
    all_to_all x2, blocking collectives, exchange(): return lax.all_to_all(value, axis, split_axis=0, concat_axis=0, tiled=True)  31.7 us
    all_to_all x4, starting transfers between devices, exchange(): return lax.all_to_all(value, axis, split_axis=0, concat_axis=0, tiled=True)  28.2 us
    ppermute x7, starting transfers between devices, shifted(): return lax.ppermute(value, axis, pairs)  26.5 us
    ppermute x7, waiting for transfers between devices, shifted(): return lax.ppermute(value, axis, pairs)  16.2 us
    all_to_all x4, waiting for transfers between devices, exchange(): return lax.all_to_all(value, axis, split_axis=0, concat_axis=0, tiled=True)  7.6 us
  transfers between devices with their start and end apart: 11, of which 7 were waited for; matrix products, arithmetic and copies ran while one was open for 4% of the time, Pallas kernels for 2%

profile of v4, /device:TPU:6, one launch (start us, length us, event | category | flops | bytes accessed | tf_op | source)
XLA Modules:
  0.0 124.1 jit_solution(11458418482461780268)
XLA Ops:
  0.0 0.0 copy-start
  0.0 1.6 %broadcast_in_dim.17 = bf16[8,32,512]{2,1,0:T(8,128)(2,1)} broadcast(bf16[32,512]{1,0:T(8,128)(2,1)} %bitcast.45), dimensions={1,2} | broadcast | bytes 294912 | tf_op jit(solution)/shard_map/broadcast_in_dim | solution.py:19
  1.6 10.3 %all-to-all-start = ((bf16[8,32,512]{2,1,0:T(8,128)(2,1)}), bf16[8,32,512]{2,1,0:T(8,128)(2,1)S(1)}, u32[]{:S(2)}, u32[]{:S(2)}) async-start(bf16[8,32,512]{2,1,0:T(8,128)(2,1)} %broadcast_in_dim.17), calls=%async_computation | async-start | bytes 524288 | tf_op jit(solution)/shard_map/all_to_all | solution.py:15
  11.9 6.9 %collective-permute-start = (bf16[2,8192]{1,0:T(2,128)(2,1)}, bf16[2,8192]{1,0:T(2,128)(2,1)}, u32[]{:S(2)}, u32[]{:S(2)}) collective-permute-start(bf16[2,8192]{1,0:T(2,128)(2,1)} %bitcast.46), channel_id=1, source_target_pairs={{0,384},{128,0},{256,128},{384,256},{1,385},{129,1},{257,129},{385... | collective-permute-start | bytes 98312 | tf_op jit(solution)/shard_map/ppermute | solution.py:25
  18.9 4.9 %all-to-all-done = bf16[8,32,512]{2,1,0:T(8,128)(2,1)S(1)} async-done(((bf16[8,32,512]{2,1,0:T(8,128)(2,1)}), bf16[8,32,512]{2,1,0:T(8,128)(2,1)S(1)}, u32[]{:S(2)}, u32[]{:S(2)}) %all-to-all-start) | async-done | bytes 262176 | tf_op jit(solution)/shard_map/all_to_all | solution.py:15
  23.8 0.0 copy-done
  23.8 0.7 convolution_convert_fusion
  24.5 0.0 collective-permute-done
  24.6 7.8 %all-to-all-start.1 = ((bf16[16,2,512]{2,1,0:T(2,128)(2,1)}), bf16[16,2,512]{2,1,0:T(2,128)(2,1)S(1)}, u32[]{:S(2)}, u32[]{:S(2)}) async-start(bf16[16,2,512]{2,1,0:T(2,128)(2,1)} %bitcast.5), calls=%async_computation.1 | async-start | bytes 65536 | tf_op jit(solution)/shard_map/all_to_all | solution.py:15
  32.4 0.9 dynamic-slice_bitcast_fusion.2
  33.3 2.0 %collective-permute-start.1 = (bf16[64,2048]{1,0:T(8,128)(2,1)}, bf16[64,2048]{1,0:T(8,128)(2,1)}, u32[]{:S(2)}, u32[]{:S(2)}) collective-permute-start(bf16[64,2048]{1,0:T(8,128)(2,1)} %get-tuple-element.19), channel_id=1, source_target_pairs={{0,4},{4,8},{8,12},{12,0},{1,5},{5,9},{9,13},{13,1},{2,6},{6,10},{... | collective-permute-start | bytes 786440 | tf_op jit(solution)/shard_map/ppermute | solution.py:25
  35.3 4.7 %collective-permute-start.2 = (bf16[64,2048]{1,0:T(8,128)(2,1)}, bf16[64,2048]{1,0:T(8,128)(2,1)}, u32[]{:S(2)}, u32[]{:S(2)}) collective-permute-start(bf16[64,2048]{1,0:T(8,128)(2,1)} %get-tuple-element.21), channel_id=1, source_target_pairs={{0,8},{4,12},{8,0},{12,4},{1,9},{5,13},{9,1},{13,5},{2,10},{6,14},... | collective-permute-start | bytes 786440 | tf_op jit(solution)/shard_map/ppermute | solution.py:25
  40.1 1.9 %collective-permute-start.3 = (bf16[64,2048]{1,0:T(8,128)(2,1)}, bf16[64,2048]{1,0:T(8,128)(2,1)}, u32[]{:S(2)}, u32[]{:S(2)}) collective-permute-start(bf16[64,2048]{1,0:T(8,128)(2,1)} %get-tuple-element.20), channel_id=1, source_target_pairs={{0,12},{4,0},{8,4},{12,8},{1,13},{5,1},{9,5},{13,9},{2,14},{6,2},{... | collective-permute-start | bytes 786440 | tf_op jit(solution)/shard_map/ppermute | solution.py:25
  42.0 0.0 all-to-all-done.1
  42.0 0.8 shard_map.46
  42.8 3.4 %all-to-all-start.2 = ((bf16[8,32,512]{2,1,0:T(8,128)(2,1)}), bf16[8,32,512]{2,1,0:T(8,128)(2,1)S(1)}, u32[]{:S(2)}, u32[]{:S(2)}) async-start(bf16[8,32,512]{2,1,0:T(8,128)(2,1)} %shard_map.46), calls=%async_computation.2 | async-start | bytes 524288 | tf_op jit(solution)/shard_map/all_to_all | solution.py:15
  46.2 0.0 collective-permute-done.1
  46.3 1.7 %collective-permute-done.2 = bf16[64,2048]{1,0:T(8,128)(2,1)} collective-permute-done((bf16[64,2048]{1,0:T(8,128)(2,1)}, bf16[64,2048]{1,0:T(8,128)(2,1)}, u32[]{:S(2)}, u32[]{:S(2)}) %collective-permute-start.2) | collective-permute-done | bytes 262176 | tf_op jit(solution)/shard_map/ppermute | solution.py:25
  47.9 3.1 %collective-permute-done.3 = bf16[64,2048]{1,0:T(8,128)(2,1)} collective-permute-done((bf16[64,2048]{1,0:T(8,128)(2,1)}, bf16[64,2048]{1,0:T(8,128)(2,1)}, u32[]{:S(2)}, u32[]{:S(2)}) %collective-permute-start.3) | collective-permute-done | bytes 262176 | tf_op jit(solution)/shard_map/ppermute | solution.py:25
  51.0 1.2 %fusion.8 = bf16[64,2048]{1,0:T(8,128)(2,1)S(1)} fusion(bf16[64,2048]{1,0:T(8,128)(2,1)} %collective-permute-done.3, bf16[64,2048]{1,0:T(8,128)(2,1)} %collective-permute-done.2, bf16[64,2048]{1,0:T(8,128)(2,1)} %collective-permute-done.1, bf16[4,64,2048]{2,1,0:T(8,128)(2,1)S(1)} %bitcast.40, s32[]{:T(128)S(6)} %select_n.48), kind=kLoop, calls=%fused_computation.8 | loop fusion | flops 1048576 | bytes 1310724 | tf_op jit(solution)/shard_map/convert_element_type | solution.py:123
  52.3 0.7 dynamic-slice_bitcast_fusion.3
  53.0 3.8 %collective-permute-start.4 = (bf16[32,2048]{1,0:T(8,128)(2,1)S(1)}, bf16[32,2048]{1,0:T(8,128)(2,1)}, u32[]{:S(2)}, u32[]{:S(2)}) collective-permute-start(bf16[32,2048]{1,0:T(8,128)(2,1)S(1)} %get-tuple-element.22), channel_id=1, source_target_pairs={{0,1},{1,0},{2,3},{3,2},{4,5},{5,4},{6,7},{7,6},{8,9},{9,8},{10,11... | collective-permute-start | bytes 393224 | tf_op jit(solution)/shard_map/ppermute | solution.py:25
  56.7 0.3 all-to-all-done.2
  57.1 0.0 copy-start.1
  57.1 1.6 %copy-done.1 = bf16[1,2048,512]{2,1,0:T(8,128)(2,1)S(1)} copy-done((bf16[1,2048,512]{2,1,0:T(8,128)(2,1)S(1)}, bf16[1,2048,512]{2,1,0:T(8,128)(2,1)}, u32[]{:S(2)}) %copy-start.1) | copy-done | bytes 2097176
  58.7 1.8 %shard_map.47 = bf16[256,2048]{1,0:T(8,128)(2,1)} custom-call(bf16[256,512]{1,0:T(8,128)(2,1)S(1)} %bitcast.37, bf16[2048,512]{1,0:T(8,128)(2,1)S(1)} %bitcast.38), custom_call_target="tpu_custom_call" | custom-call | flops 20000000000 | bytes 1048576 | tf_op jit(solution)/shard_map/pallas_call | solution.py:93
  60.4 0.0 copy-start.2
  60.4 0.0 collective-permute-done.4
  60.4 6.6 %all-to-all-start.3 = ((bf16[8,32,2048]{2,1,0:T(8,128)(2,1)}), bf16[8,32,2048]{2,1,0:T(8,128)(2,1)S(1)}, u32[]{:S(2)}, u32[]{:S(2)}) async-start(bf16[8,32,2048]{2,1,0:T(8,128)(2,1)} %bitcast.16), calls=%async_computation.3 | async-start | bytes 2097152 | tf_op jit(solution)/shard_map/all_to_all | solution.py:15
  67.0 0.0 copy-done.2
  67.0 0.9 add_convert_fusion
  67.9 4.3 %collective-permute-start.5 = (bf16[32,2048]{1,0:T(8,128)(2,1)S(1)}, bf16[32,2048]{1,0:T(8,128)(2,1)S(1)}, u32[]{:S(2)}, u32[]{:S(2)}) collective-permute-start(bf16[32,2048]{1,0:T(8,128)(2,1)S(1)} %add_convert_fusion), channel_id=1, source_target_pairs={{0,2},{2,0},{1,3},{3,1},{4,6},{6,4},{5,7},{7,5},{8,10},{10,8},{9,1... | collective-permute-start | bytes 393224 | tf_op jit(solution)/shard_map/ppermute | solution.py:25
  72.2 6.4 %collective-permute-done.5 = bf16[32,2048]{1,0:T(8,128)(2,1)S(1)} collective-permute-done((bf16[32,2048]{1,0:T(8,128)(2,1)S(1)}, bf16[32,2048]{1,0:T(8,128)(2,1)S(1)}, u32[]{:S(2)}, u32[]{:S(2)}) %collective-permute-start.5) | collective-permute-done | bytes 131104 | tf_op jit(solution)/shard_map/ppermute | solution.py:25
  78.6 0.2 fusion.13
  78.8 2.4 %all-to-all-done.3 = bf16[8,32,2048]{2,1,0:T(8,128)(2,1)S(1)} async-done(((bf16[8,32,2048]{2,1,0:T(8,128)(2,1)}), bf16[8,32,2048]{2,1,0:T(8,128)(2,1)S(1)}, u32[]{:S(2)}, u32[]{:S(2)}) %all-to-all-start.3) | async-done | bytes 1048608 | tf_op jit(solution)/shard_map/all_to_all | solution.py:15
  81.2 0.8 reduce_sum.21
  82.0 2.9 %collective-permute-start.6 = (bf16[32,2048]{1,0:T(8,128)(2,1)}, bf16[32,2048]{1,0:T(8,128)(2,1)S(1)}, u32[]{:S(2)}, u32[]{:S(2)}) collective-permute-start(bf16[32,2048]{1,0:T(8,128)(2,1)} %reduce_sum.21), channel_id=1, source_target_pairs={{0,2},{2,0},{1,3},{3,1},{4,6},{6,4},{5,7},{7,5},{8,10},{10,8},{9,1... | collective-permute-start | bytes 393224 | tf_op jit(solution)/shard_map/ppermute | solution.py:25
  84.9 5.0 %collective-permute-done.6 = bf16[32,2048]{1,0:T(8,128)(2,1)S(1)} collective-permute-done((bf16[32,2048]{1,0:T(8,128)(2,1)}, bf16[32,2048]{1,0:T(8,128)(2,1)S(1)}, u32[]{:S(2)}, u32[]{:S(2)}) %collective-permute-start.6) | collective-permute-done | bytes 131104 | tf_op jit(solution)/shard_map/ppermute | solution.py:25
  89.9 1.0 multiply_convert_fusion
  90.9 0.1 broadcast_in_dim.18
  91.0 15.1 %all_to_all.30 = bf16[8,32,2048]{2,1,0:T(8,128)(2,1)S(1)} all-to-all(bf16[8,32,2048]{2,1,0:T(8,128)(2,1)S(1)} %broadcast_in_dim.18), channel_id=1, replica_groups=mesh['section'=4,'dp'=8,'tx'=4,'ty1'=2,'ty0'=2] {'tx','ty0'}, dimensions={0} | all-to-all | bytes 2097152 | tf_op jit(solution)/shard_map/all_to_all | solution.py:15
  106.2 0.7 fusion.3
  106.9 16.5 %all_to_all.31 = bf16[8,32,512]{2,1,0:T(8,128)(2,1)S(1)} all-to-all(bf16[8,32,512]{2,1,0:T(8,128)(2,1)S(1)} %bitcast.44), channel_id=1, replica_groups=mesh['section'=4,'dp'=8,'tx'=4,'ty1'=2,'ty0'=2] {'dp'}, dimensions={0} | all-to-all | bytes 524288 | tf_op jit(solution)/shard_map/all_to_all | solution.py:15
  123.5 0.6 fusion.14
  (2 shorter events, 0.1 us)
Async XLA Ops:
  0.0 23.8 %copy-start = (bf16[1,512,2048]{2,1,0:T(8,128)(2,1)S(1)}, bf16[1,512,2048]{2,1,0:T(8,128)(2,1)}, u32[]{:S(2)}) copy-start(bf16[1,512,2048]{2,1,0:T(8,128)(2,1)} %param.5) | copy-start | bytes 6291460
  1.6 22.2 %all-to-all-start = ((bf16[8,32,512]{2,1,0:T(8,128)(2,1)}), bf16[8,32,512]{2,1,0:T(8,128)(2,1)S(1)}, u32[]{:S(2)}, u32[]{:S(2)}) async-start(bf16[8,32,512]{2,1,0:T(8,128)(2,1)} %broadcast_in_dim.17), calls=%async_computation | async-start | bytes 524288 | tf_op jit(solution)/shard_map/all_to_all | solution.py:15
  11.9 12.6 %collective-permute-start = (bf16[2,8192]{1,0:T(2,128)(2,1)}, bf16[2,8192]{1,0:T(2,128)(2,1)}, u32[]{:S(2)}, u32[]{:S(2)}) collective-permute-start(bf16[2,8192]{1,0:T(2,128)(2,1)} %bitcast.46), channel_id=1, source_target_pairs={{0,384},{128,0},{256,128},{384,256},{1,385},{129,1},{257,129},{385... | collective-permute-start | bytes 98312 | tf_op jit(solution)/shard_map/ppermute | solution.py:25
  24.6 17.4 %all-to-all-start.1 = ((bf16[16,2,512]{2,1,0:T(2,128)(2,1)}), bf16[16,2,512]{2,1,0:T(2,128)(2,1)S(1)}, u32[]{:S(2)}, u32[]{:S(2)}) async-start(bf16[16,2,512]{2,1,0:T(2,128)(2,1)} %bitcast.5), calls=%async_computation.1 | async-start | bytes 65536 | tf_op jit(solution)/shard_map/all_to_all | solution.py:15
  33.3 12.9 %collective-permute-start.1 = (bf16[64,2048]{1,0:T(8,128)(2,1)}, bf16[64,2048]{1,0:T(8,128)(2,1)}, u32[]{:S(2)}, u32[]{:S(2)}) collective-permute-start(bf16[64,2048]{1,0:T(8,128)(2,1)} %get-tuple-element.19), channel_id=1, source_target_pairs={{0,4},{4,8},{8,12},{12,0},{1,5},{5,9},{9,13},{13,1},{2,6},{6,10},{... | collective-permute-start | bytes 786440 | tf_op jit(solution)/shard_map/ppermute | solution.py:25
  35.3 12.6 %collective-permute-start.2 = (bf16[64,2048]{1,0:T(8,128)(2,1)}, bf16[64,2048]{1,0:T(8,128)(2,1)}, u32[]{:S(2)}, u32[]{:S(2)}) collective-permute-start(bf16[64,2048]{1,0:T(8,128)(2,1)} %get-tuple-element.21), channel_id=1, source_target_pairs={{0,8},{4,12},{8,0},{12,4},{1,9},{5,13},{9,1},{13,5},{2,10},{6,14},... | collective-permute-start | bytes 786440 | tf_op jit(solution)/shard_map/ppermute | solution.py:25
  40.1 11.0 %collective-permute-start.3 = (bf16[64,2048]{1,0:T(8,128)(2,1)}, bf16[64,2048]{1,0:T(8,128)(2,1)}, u32[]{:S(2)}, u32[]{:S(2)}) collective-permute-start(bf16[64,2048]{1,0:T(8,128)(2,1)} %get-tuple-element.20), channel_id=1, source_target_pairs={{0,12},{4,0},{8,4},{12,8},{1,13},{5,1},{9,5},{13,9},{2,14},{6,2},{... | collective-permute-start | bytes 786440 | tf_op jit(solution)/shard_map/ppermute | solution.py:25
  42.8 14.2 %all-to-all-start.2 = ((bf16[8,32,512]{2,1,0:T(8,128)(2,1)}), bf16[8,32,512]{2,1,0:T(8,128)(2,1)S(1)}, u32[]{:S(2)}, u32[]{:S(2)}) async-start(bf16[8,32,512]{2,1,0:T(8,128)(2,1)} %shard_map.46), calls=%async_computation.2 | async-start | bytes 524288 | tf_op jit(solution)/shard_map/all_to_all | solution.py:15
  53.0 7.5 %collective-permute-start.4 = (bf16[32,2048]{1,0:T(8,128)(2,1)S(1)}, bf16[32,2048]{1,0:T(8,128)(2,1)}, u32[]{:S(2)}, u32[]{:S(2)}) collective-permute-start(bf16[32,2048]{1,0:T(8,128)(2,1)S(1)} %get-tuple-element.22), channel_id=1, source_target_pairs={{0,1},{1,0},{2,3},{3,2},{4,5},{5,4},{6,7},{7,6},{8,9},{9,8},{10,11... | collective-permute-start | bytes 393224 | tf_op jit(solution)/shard_map/ppermute | solution.py:25
  57.1 1.6 %copy-start.1 = (bf16[1,2048,512]{2,1,0:T(8,128)(2,1)S(1)}, bf16[1,2048,512]{2,1,0:T(8,128)(2,1)}, u32[]{:S(2)}) copy-start(bf16[1,2048,512]{2,1,0:T(8,128)(2,1)} %param.6) | copy-start | bytes 6291460
  60.4 6.6 %copy-start.2 = (bf16[32,2048]{1,0:T(8,128)(2,1)S(1)}, bf16[32,2048]{1,0:T(8,128)(2,1)}, u32[]{:S(2)}) copy-start(bf16[32,2048]{1,0:T(8,128)(2,1)} %get-tuple-element.15) | copy-start | bytes 393220
  60.4 20.7 %all-to-all-start.3 = ((bf16[8,32,2048]{2,1,0:T(8,128)(2,1)}), bf16[8,32,2048]{2,1,0:T(8,128)(2,1)S(1)}, u32[]{:S(2)}, u32[]{:S(2)}) async-start(bf16[8,32,2048]{2,1,0:T(8,128)(2,1)} %bitcast.16), calls=%async_computation.3 | async-start | bytes 2097152 | tf_op jit(solution)/shard_map/all_to_all | solution.py:15
  67.9 10.7 %collective-permute-start.5 = (bf16[32,2048]{1,0:T(8,128)(2,1)S(1)}, bf16[32,2048]{1,0:T(8,128)(2,1)S(1)}, u32[]{:S(2)}, u32[]{:S(2)}) collective-permute-start(bf16[32,2048]{1,0:T(8,128)(2,1)S(1)} %add_convert_fusion), channel_id=1, source_target_pairs={{0,2},{2,0},{1,3},{3,1},{4,6},{6,4},{5,7},{7,5},{8,10},{10,8},{9,1... | collective-permute-start | bytes 393224 | tf_op jit(solution)/shard_map/ppermute | solution.py:25
  82.0 8.0 %collective-permute-start.6 = (bf16[32,2048]{1,0:T(8,128)(2,1)}, bf16[32,2048]{1,0:T(8,128)(2,1)S(1)}, u32[]{:S(2)}, u32[]{:S(2)}) collective-permute-start(bf16[32,2048]{1,0:T(8,128)(2,1)} %reduce_sum.21), channel_id=1, source_target_pairs={{0,2},{2,0},{1,3},{3,1},{4,6},{6,4},{5,7},{7,5},{8,10},{10,8},{9,1... | collective-permute-start | bytes 393224 | tf_op jit(solution)/shard_map/ppermute | solution.py:25

commit v5 on v4

--- a/solution.py
+++ b/solution.py
@@ -76,28 +76,56 @@
     )(value)
 
 
-def turned_dot_kernel(left_ref, right_ref, out_ref):
-    step = 512
-    for begin in range(0, out_ref.shape[1], step):
-        out_ref[:, begin : begin + step] = lax.dot_general(
+def turned_dot_kernel(left_ref, right_hbm, out_hbm, right_ref, out_ref, sems, out_sems):
+    parts, step = right_ref.shape[:2]
+    fetches = [
+        pltpu.make_async_copy(
+            right_hbm.at[pl.ds(at * step, step)], right_ref.at[at], sems.at[at]
+        )
+        for at in range(parts)
+    ]
+    stores = [
+        pltpu.make_async_copy(
+            out_ref.at[at], out_hbm.at[:, pl.ds(at * step, step)], out_sems.at[at]
+        )
+        for at in range(parts)
+    ]
+    for fetch in fetches:
+        fetch.start()
+    for at in range(parts):
+        fetches[at].wait()
+        out_ref[at] = lax.dot_general(
             left_ref[...],
-            right_ref[begin : begin + step, :],
+            right_ref[at],
             (((1,), (1,)), ((), ())),
             preferred_element_type=jnp.float32,
         ).astype(out_ref.dtype)
+        stores[at].start()
+    for store in stores:
+        store.wait()
 
 
 def turned_dot(left, right):
+    parts = 4
     rows, units = left.shape[0], right.shape[0]
-    vmem = pl.BlockSpec(memory_space=pltpu.VMEM)
+    step = units // parts
     return pl.pallas_call(
         turned_dot_kernel,
         out_shape=jax.ShapeDtypeStruct((rows, units), jnp.bfloat16),
-        in_specs=[vmem, vmem],
-        out_specs=vmem,
+        in_specs=[
+            pl.BlockSpec(memory_space=pltpu.VMEM),
+            pl.BlockSpec(memory_space=pl.ANY),
+        ],
+        out_specs=pl.BlockSpec(memory_space=pl.ANY),
+        scratch_shapes=[
+            pltpu.VMEM((parts, step, right.shape[1]), right.dtype),
+            pltpu.VMEM((parts, rows, step), jnp.bfloat16),
+            pltpu.SemaphoreType.DMA((parts,)),
+            pltpu.SemaphoreType.DMA((parts,)),
+        ],
         compiler_params=pltpu.CompilerParams(vmem_limit_bytes=8 * 2**20),
         cost_estimate=LONG,
-    )(left, pltpu.with_memory_space_constraint(right, pltpu.VMEM))
+    )(left, pltpu.with_memory_space_constraint(right, pltpu.HBM))
 
 
 def per_device(saved_input, w_up, w_down, sent_grad):
@@ -129,9 +157,11 @@
     back_near = jnp.sum(
         exchange(back_part.reshape(near, -1, units), NEAR).astype(jnp.float32), axis=0
     ).astype(jnp.bfloat16)
-    slope = gelu_slope(block_sum([hidden, shifted(hidden, "ty1", 1)]))
-    back_near, slope = lax.optimization_barrier((back_near, slope))
+    hidden_far = shifted(hidden, "ty1", 1)
+    back_near, hidden_far = lax.optimization_barrier((back_near, hidden_far))
+    slope = gelu_slope(block_sum([hidden, hidden_far]))
     back_far = shifted(back_near, "ty1", 1)
+    back_far, slope = lax.optimization_barrier((back_far, slope))
     back_hidden = back_near.astype(jnp.float32) + back_far.astype(jnp.float32)
     slope_grad = (back_hidden * slope).astype(jnp.bfloat16)
     slope_grad = exchange(copies(slope_grad, NEAR), NEAR).reshape(-1, units)

time: 126 us -> 126 us (level)
  blocking collectives: 31.7 us -> 29.9 us
  local copies, waits for them, and re-layouts: 4.95 us -> 3.36 us
  Pallas kernels: 2.53 us -> 3.98 us
    all_to_all x4, waiting for transfers between devices: 7.6 us -> 14.2 us  [exchange(): return lax.all_to_all(value, axis, split_axis=0, concat_axis=0, tiled=True)]
    ppermute x7, waiting for transfers between devices: 16.2 us -> 10.4 us  [shifted(): return lax.ppermute(value, axis, pairs)]
    all_to_all x2, blocking collectives: 31.7 us -> 29.9 us  [exchange(): return lax.all_to_all(value, axis, split_axis=0, concat_axis=0, tiled=True)]
    unnamed x6, local copies, waits for them, and re-layouts: 1.6 us -> 0.01 us
    pallas_call x1, Pallas kernels: 1.75 us -> 3.21 us  [turned_dot(): pl.pallas_call(turned_dot_kernel, out_shape=jax.ShapeDtypeStruct((rows, u...]
  transfers between devices with their start and end apart: 11 -> 11, of which waited for: 7 -> 6; matrix products, arithmetic and copies ran while one was open for 4% -> 5% of each run, Pallas kernels for 2% -> 3%
where the time goes in v5:
time: 126 us; the launch traced here: 124 us
  starting transfers between devices  54.3 us (43%)
  blocking collectives  29.9 us (24%)
  waiting for transfers between devices  24.6 us (20%)
  other arithmetic  5.76 us (5%)
  Pallas kernels  3.98 us (3%)
  local copies, waits for them, and re-layouts  3.36 us (3%)
  matrix products  1.46 us (1%)
    all_to_all x2, blocking collectives, exchange(): return lax.all_to_all(value, axis, split_axis=0, concat_axis=0, tiled=True)  29.9 us
    all_to_all x4, starting transfers between devices, exchange(): return lax.all_to_all(value, axis, split_axis=0, concat_axis=0, tiled=True)  28.2 us
    ppermute x7, starting transfers between devices, shifted(): return lax.ppermute(value, axis, pairs)  26.1 us
    all_to_all x4, waiting for transfers between devices, exchange(): return lax.all_to_all(value, axis, split_axis=0, concat_axis=0, tiled=True)  14.2 us
    ppermute x7, waiting for transfers between devices, shifted(): return lax.ppermute(value, axis, pairs)  10.4 us
    pallas_call x1, Pallas kernels, turned_dot(): pl.pallas_call(turned_dot_kernel, out_shape=jax.ShapeDtypeStruct((rows, u...  3.21 us
  transfers between devices with their start and end apart: 11, of which 6 were waited for; matrix products, arithmetic and copies ran while one was open for 5% of the time, Pallas kernels for 3%

profile of v5, /device:TPU:6, one launch (start us, length us, event | category | flops | bytes accessed | tf_op | source)
XLA Modules:
  0.0 123.6 jit_solution(9274219805349820475)
XLA Ops:
  0.0 0.0 copy-start
  0.0 1.6 %broadcast_in_dim.17 = bf16[8,32,512]{2,1,0:T(8,128)(2,1)} broadcast(bf16[32,512]{1,0:T(8,128)(2,1)} %bitcast.44), dimensions={1,2} | broadcast | bytes 294912 | tf_op jit(solution)/shard_map/broadcast_in_dim | solution.py:19
  1.6 10.3 %all-to-all-start = ((bf16[8,32,512]{2,1,0:T(8,128)(2,1)}), bf16[8,32,512]{2,1,0:T(8,128)(2,1)S(1)}, u32[]{:S(2)}, u32[]{:S(2)}) async-start(bf16[8,32,512]{2,1,0:T(8,128)(2,1)} %broadcast_in_dim.17), calls=%async_computation | async-start | bytes 524288 | tf_op jit(solution)/shard_map/all_to_all | solution.py:15
  11.9 6.9 %collective-permute-start = (bf16[2,8192]{1,0:T(2,128)(2,1)}, bf16[2,8192]{1,0:T(2,128)(2,1)}, u32[]{:S(2)}, u32[]{:S(2)}) collective-permute-start(bf16[2,8192]{1,0:T(2,128)(2,1)} %bitcast.46), channel_id=1, source_target_pairs={{0,384},{128,0},{256,128},{384,256},{1,385},{129,1},{257,129},{385... | collective-permute-start | bytes 98312 | tf_op jit(solution)/shard_map/ppermute | solution.py:25
  18.9 4.9 %all-to-all-done = bf16[8,32,512]{2,1,0:T(8,128)(2,1)S(1)} async-done(((bf16[8,32,512]{2,1,0:T(8,128)(2,1)}), bf16[8,32,512]{2,1,0:T(8,128)(2,1)S(1)}, u32[]{:S(2)}, u32[]{:S(2)}) %all-to-all-start) | async-done | bytes 262176 | tf_op jit(solution)/shard_map/all_to_all | solution.py:15
  23.8 0.0 copy-done
  23.8 0.7 convolution_convert_fusion
  24.5 0.0 collective-permute-done
  24.6 7.8 %all-to-all-start.1 = ((bf16[16,2,512]{2,1,0:T(2,128)(2,1)}), bf16[16,2,512]{2,1,0:T(2,128)(2,1)S(1)}, u32[]{:S(2)}, u32[]{:S(2)}) async-start(bf16[16,2,512]{2,1,0:T(2,128)(2,1)} %bitcast.5), calls=%async_computation.1 | async-start | bytes 65536 | tf_op jit(solution)/shard_map/all_to_all | solution.py:15
  32.4 0.9 dynamic-slice_bitcast_fusion.2
  33.3 2.0 %collective-permute-start.1 = (bf16[64,2048]{1,0:T(8,128)(2,1)}, bf16[64,2048]{1,0:T(8,128)(2,1)}, u32[]{:S(2)}, u32[]{:S(2)}) collective-permute-start(bf16[64,2048]{1,0:T(8,128)(2,1)} %get-tuple-element.23), channel_id=1, source_target_pairs={{0,4},{4,8},{8,12},{12,0},{1,5},{5,9},{9,13},{13,1},{2,6},{6,10},{... | collective-permute-start | bytes 786440 | tf_op jit(solution)/shard_map/ppermute | solution.py:25
  35.3 4.7 %collective-permute-start.2 = (bf16[64,2048]{1,0:T(8,128)(2,1)}, bf16[64,2048]{1,0:T(8,128)(2,1)}, u32[]{:S(2)}, u32[]{:S(2)}) collective-permute-start(bf16[64,2048]{1,0:T(8,128)(2,1)} %get-tuple-element.25), channel_id=1, source_target_pairs={{0,8},{4,12},{8,0},{12,4},{1,9},{5,13},{9,1},{13,5},{2,10},{6,14},... | collective-permute-start | bytes 786440 | tf_op jit(solution)/shard_map/ppermute | solution.py:25
  40.1 1.9 %collective-permute-start.3 = (bf16[64,2048]{1,0:T(8,128)(2,1)}, bf16[64,2048]{1,0:T(8,128)(2,1)}, u32[]{:S(2)}, u32[]{:S(2)}) collective-permute-start(bf16[64,2048]{1,0:T(8,128)(2,1)} %get-tuple-element.24), channel_id=1, source_target_pairs={{0,12},{4,0},{8,4},{12,8},{1,13},{5,1},{9,5},{13,9},{2,14},{6,2},{... | collective-permute-start | bytes 786440 | tf_op jit(solution)/shard_map/ppermute | solution.py:25
  42.0 0.0 all-to-all-done.1
  42.0 0.8 shard_map.46
  42.8 3.4 %all-to-all-start.2 = ((bf16[8,32,512]{2,1,0:T(8,128)(2,1)}), bf16[8,32,512]{2,1,0:T(8,128)(2,1)S(1)}, u32[]{:S(2)}, u32[]{:S(2)}) async-start(bf16[8,32,512]{2,1,0:T(8,128)(2,1)} %shard_map.46), calls=%async_computation.2 | async-start | bytes 524288 | tf_op jit(solution)/shard_map/all_to_all | solution.py:15
  46.2 0.0 collective-permute-done.1
  46.3 1.7 %collective-permute-done.2 = bf16[64,2048]{1,0:T(8,128)(2,1)} collective-permute-done((bf16[64,2048]{1,0:T(8,128)(2,1)}, bf16[64,2048]{1,0:T(8,128)(2,1)}, u32[]{:S(2)}, u32[]{:S(2)}) %collective-permute-start.2) | collective-permute-done | bytes 262176 | tf_op jit(solution)/shard_map/ppermute | solution.py:25
  47.9 3.1 %collective-permute-done.3 = bf16[64,2048]{1,0:T(8,128)(2,1)} collective-permute-done((bf16[64,2048]{1,0:T(8,128)(2,1)}, bf16[64,2048]{1,0:T(8,128)(2,1)}, u32[]{:S(2)}, u32[]{:S(2)}) %collective-permute-start.3) | collective-permute-done | bytes 262176 | tf_op jit(solution)/shard_map/ppermute | solution.py:25
  51.0 1.2 %fusion.8 = bf16[64,2048]{1,0:T(8,128)(2,1)S(1)} fusion(bf16[64,2048]{1,0:T(8,128)(2,1)} %collective-permute-done.3, bf16[64,2048]{1,0:T(8,128)(2,1)} %collective-permute-done.2, bf16[64,2048]{1,0:T(8,128)(2,1)} %collective-permute-done.1, bf16[4,64,2048]{2,1,0:T(8,128)(2,1)S(1)} %bitcast.39, s32[]{:T(128)S(6)} %select_n.48), kind=kLoop, calls=%fused_computation.8 | loop fusion | flops 1048576 | bytes 1310724 | tf_op jit(solution)/shard_map/convert_element_type | solution.py:151
  52.3 0.7 dynamic-slice_bitcast_fusion.3
  53.0 3.8 %collective-permute-start.4 = (bf16[32,2048]{1,0:T(8,128)(2,1)S(1)}, bf16[32,2048]{1,0:T(8,128)(2,1)}, u32[]{:S(2)}, u32[]{:S(2)}) collective-permute-start(bf16[32,2048]{1,0:T(8,128)(2,1)S(1)} %get-tuple-element.26), channel_id=1, source_target_pairs={{0,1},{1,0},{2,3},{3,2},{4,5},{5,4},{6,7},{7,6},{8,9},{9,8},{10,11... | collective-permute-start | bytes 393224 | tf_op jit(solution)/shard_map/ppermute | solution.py:25
  56.7 0.3 all-to-all-done.2
  57.1 3.2 %shard_map.47 = bf16[256,2048]{1,0:T(8,128)(2,1)} custom-call(bf16[256,512]{1,0:T(8,128)(2,1)S(1)} %bitcast.37, bf16[2048,512]{1,0:T(8,128)(2,1)} %bitcast.45), custom_call_target="tpu_custom_call" | custom-call | flops 20000000000 | bytes 1048576 | tf_op jit(solution)/shard_map/pallas_call | solution.py:112
  60.3 0.0 copy-start.1
  60.3 0.0 collective-permute-done.4
  60.3 6.6 %all-to-all-start.3 = ((bf16[8,32,2048]{2,1,0:T(8,128)(2,1)}), bf16[8,32,2048]{2,1,0:T(8,128)(2,1)S(1)}, u32[]{:S(2)}, u32[]{:S(2)}) async-start(bf16[8,32,2048]{2,1,0:T(8,128)(2,1)} %bitcast.16), calls=%async_computation.3 | async-start | bytes 2097152 | tf_op jit(solution)/shard_map/all_to_all | solution.py:15
  66.9 0.0 copy-done.1
  66.9 0.9 add_convert_fusion
  67.8 0.0 copy-start.2
  67.8 4.3 %collective-permute-start.5 = (bf16[32,2048]{1,0:T(8,128)(2,1)S(1)}, bf16[32,2048]{1,0:T(8,128)(2,1)}, u32[]{:S(2)}, u32[]{:S(2)}) collective-permute-start(bf16[32,2048]{1,0:T(8,128)(2,1)S(1)} %add_convert_fusion), channel_id=1, source_target_pairs={{0,2},{2,0},{1,3},{3,1},{4,6},{6,4},{5,7},{7,5},{8,10},{10,8},{9,1... | collective-permute-start | bytes 393224 | tf_op jit(solution)/shard_map/ppermute | solution.py:25
  72.1 9.0 %all-to-all-done.3 = bf16[8,32,2048]{2,1,0:T(8,128)(2,1)S(1)} async-done(((bf16[8,32,2048]{2,1,0:T(8,128)(2,1)}), bf16[8,32,2048]{2,1,0:T(8,128)(2,1)S(1)}, u32[]{:S(2)}, u32[]{:S(2)}) %all-to-all-start.3) | async-done | bytes 1048608 | tf_op jit(solution)/shard_map/all_to_all | solution.py:15
  81.1 0.8 reduce_sum.21
  81.9 0.0 collective-permute-done.5
  81.9 0.0 copy-done.2
  81.9 2.6 %collective-permute-start.6 = (bf16[32,2048]{1,0:T(8,128)(2,1)}, bf16[32,2048]{1,0:T(8,128)(2,1)S(1)}, u32[]{:S(2)}, u32[]{:S(2)}) collective-permute-start(bf16[32,2048]{1,0:T(8,128)(2,1)} %reduce_sum.21), channel_id=1, source_target_pairs={{0,2},{2,0},{1,3},{3,1},{4,6},{6,4},{5,7},{7,5},{8,10},{10,8},{9,1... | collective-permute-start | bytes 393224 | tf_op jit(solution)/shard_map/ppermute | solution.py:25
  84.5 1.2 fusion.13
  85.6 5.6 %collective-permute-done.6 = bf16[32,2048]{1,0:T(8,128)(2,1)S(1)} collective-permute-done((bf16[32,2048]{1,0:T(8,128)(2,1)}, bf16[32,2048]{1,0:T(8,128)(2,1)S(1)}, u32[]{:S(2)}, u32[]{:S(2)}) %collective-permute-start.6) | collective-permute-done | bytes 131104 | tf_op jit(solution)/shard_map/ppermute | solution.py:25
  91.2 1.0 multiply_convert_fusion
  92.2 0.1 broadcast_in_dim.18
  92.3 13.4 %all_to_all.30 = bf16[8,32,2048]{2,1,0:T(8,128)(2,1)S(1)} all-to-all(bf16[8,32,2048]{2,1,0:T(8,128)(2,1)S(1)} %broadcast_in_dim.18), channel_id=1, replica_groups=mesh['section'=4,'dp'=8,'tx'=4,'ty1'=2,'ty0'=2] {'tx','ty0'}, dimensions={0} | all-to-all | bytes 2097152 | tf_op jit(solution)/shard_map/all_to_all | solution.py:15
  105.7 0.7 fusion.3
  106.5 16.5 %all_to_all.31 = bf16[8,32,512]{2,1,0:T(8,128)(2,1)S(1)} all-to-all(bf16[8,32,512]{2,1,0:T(8,128)(2,1)S(1)} %bitcast.43), channel_id=1, replica_groups=mesh['section'=4,'dp'=8,'tx'=4,'ty1'=2,'ty0'=2] {'dp'}, dimensions={0} | all-to-all | bytes 524288 | tf_op jit(solution)/shard_map/all_to_all | solution.py:15
  123.0 0.6 fusion.14
  (2 shorter events, 0.1 us)
Async XLA Ops:
  0.0 23.8 %copy-start = (bf16[1,512,2048]{2,1,0:T(8,128)(2,1)S(1)}, bf16[1,512,2048]{2,1,0:T(8,128)(2,1)}, u32[]{:S(2)}) copy-start(bf16[1,512,2048]{2,1,0:T(8,128)(2,1)} %param.5) | copy-start | bytes 6291460
  1.6 22.2 %all-to-all-start = ((bf16[8,32,512]{2,1,0:T(8,128)(2,1)}), bf16[8,32,512]{2,1,0:T(8,128)(2,1)S(1)}, u32[]{:S(2)}, u32[]{:S(2)}) async-start(bf16[8,32,512]{2,1,0:T(8,128)(2,1)} %broadcast_in_dim.17), calls=%async_computation | async-start | bytes 524288 | tf_op jit(solution)/shard_map/all_to_all | solution.py:15
  11.9 12.6 %collective-permute-start = (bf16[2,8192]{1,0:T(2,128)(2,1)}, bf16[2,8192]{1,0:T(2,128)(2,1)}, u32[]{:S(2)}, u32[]{:S(2)}) collective-permute-start(bf16[2,8192]{1,0:T(2,128)(2,1)} %bitcast.46), channel_id=1, source_target_pairs={{0,384},{128,0},{256,128},{384,256},{1,385},{129,1},{257,129},{385... | collective-permute-start | bytes 98312 | tf_op jit(solution)/shard_map/ppermute | solution.py:25
  24.6 17.4 %all-to-all-start.1 = ((bf16[16,2,512]{2,1,0:T(2,128)(2,1)}), bf16[16,2,512]{2,1,0:T(2,128)(2,1)S(1)}, u32[]{:S(2)}, u32[]{:S(2)}) async-start(bf16[16,2,512]{2,1,0:T(2,128)(2,1)} %bitcast.5), calls=%async_computation.1 | async-start | bytes 65536 | tf_op jit(solution)/shard_map/all_to_all | solution.py:15
  33.3 12.9 %collective-permute-start.1 = (bf16[64,2048]{1,0:T(8,128)(2,1)}, bf16[64,2048]{1,0:T(8,128)(2,1)}, u32[]{:S(2)}, u32[]{:S(2)}) collective-permute-start(bf16[64,2048]{1,0:T(8,128)(2,1)} %get-tuple-element.23), channel_id=1, source_target_pairs={{0,4},{4,8},{8,12},{12,0},{1,5},{5,9},{9,13},{13,1},{2,6},{6,10},{... | collective-permute-start | bytes 786440 | tf_op jit(solution)/shard_map/ppermute | solution.py:25
  35.3 12.6 %collective-permute-start.2 = (bf16[64,2048]{1,0:T(8,128)(2,1)}, bf16[64,2048]{1,0:T(8,128)(2,1)}, u32[]{:S(2)}, u32[]{:S(2)}) collective-permute-start(bf16[64,2048]{1,0:T(8,128)(2,1)} %get-tuple-element.25), channel_id=1, source_target_pairs={{0,8},{4,12},{8,0},{12,4},{1,9},{5,13},{9,1},{13,5},{2,10},{6,14},... | collective-permute-start | bytes 786440 | tf_op jit(solution)/shard_map/ppermute | solution.py:25
  40.1 11.0 %collective-permute-start.3 = (bf16[64,2048]{1,0:T(8,128)(2,1)}, bf16[64,2048]{1,0:T(8,128)(2,1)}, u32[]{:S(2)}, u32[]{:S(2)}) collective-permute-start(bf16[64,2048]{1,0:T(8,128)(2,1)} %get-tuple-element.24), channel_id=1, source_target_pairs={{0,12},{4,0},{8,4},{12,8},{1,13},{5,1},{9,5},{13,9},{2,14},{6,2},{... | collective-permute-start | bytes 786440 | tf_op jit(solution)/shard_map/ppermute | solution.py:25
  42.8 14.2 %all-to-all-start.2 = ((bf16[8,32,512]{2,1,0:T(8,128)(2,1)}), bf16[8,32,512]{2,1,0:T(8,128)(2,1)S(1)}, u32[]{:S(2)}, u32[]{:S(2)}) async-start(bf16[8,32,512]{2,1,0:T(8,128)(2,1)} %shard_map.46), calls=%async_computation.2 | async-start | bytes 524288 | tf_op jit(solution)/shard_map/all_to_all | solution.py:15
  53.0 7.3 %collective-permute-start.4 = (bf16[32,2048]{1,0:T(8,128)(2,1)S(1)}, bf16[32,2048]{1,0:T(8,128)(2,1)}, u32[]{:S(2)}, u32[]{:S(2)}) collective-permute-start(bf16[32,2048]{1,0:T(8,128)(2,1)S(1)} %get-tuple-element.26), channel_id=1, source_target_pairs={{0,1},{1,0},{2,3},{3,2},{4,5},{5,4},{6,7},{7,6},{8,9},{9,8},{10,11... | collective-permute-start | bytes 393224 | tf_op jit(solution)/shard_map/ppermute | solution.py:25
  60.3 6.6 %copy-start.1 = (bf16[32,2048]{1,0:T(8,128)(2,1)S(1)}, bf16[32,2048]{1,0:T(8,128)(2,1)}, u32[]{:S(2)}) copy-start(bf16[32,2048]{1,0:T(8,128)(2,1)} %get-tuple-element.17) | copy-start | bytes 393220
  60.3 20.8 %all-to-all-start.3 = ((bf16[8,32,2048]{2,1,0:T(8,128)(2,1)}), bf16[8,32,2048]{2,1,0:T(8,128)(2,1)S(1)}, u32[]{:S(2)}, u32[]{:S(2)}) async-start(bf16[8,32,2048]{2,1,0:T(8,128)(2,1)} %bitcast.16), calls=%async_computation.3 | async-start | bytes 2097152 | tf_op jit(solution)/shard_map/all_to_all | solution.py:15
  67.8 14.1 %copy-start.2 = (bf16[32,2048]{1,0:T(8,128)(2,1)}, bf16[32,2048]{1,0:T(8,128)(2,1)S(1)}, u32[]{:S(2)}) copy-start(bf16[32,2048]{1,0:T(8,128)(2,1)S(1)} %add_convert_fusion) | copy-start | bytes 393220
  67.8 14.0 %collective-permute-start.5 = (bf16[32,2048]{1,0:T(8,128)(2,1)S(1)}, bf16[32,2048]{1,0:T(8,128)(2,1)}, u32[]{:S(2)}, u32[]{:S(2)}) collective-permute-start(bf16[32,2048]{1,0:T(8,128)(2,1)S(1)} %add_convert_fusion), channel_id=1, source_target_pairs={{0,2},{2,0},{1,3},{3,1},{4,6},{6,4},{5,7},{7,5},{8,10},{10,8},{9,1... | collective-permute-start | bytes 393224 | tf_op jit(solution)/shard_map/ppermute | solution.py:25
  81.9 9.4 %collective-permute-start.6 = (bf16[32,2048]{1,0:T(8,128)(2,1)}, bf16[32,2048]{1,0:T(8,128)(2,1)S(1)}, u32[]{:S(2)}, u32[]{:S(2)}) collective-permute-start(bf16[32,2048]{1,0:T(8,128)(2,1)} %reduce_sum.21), channel_id=1, source_target_pairs={{0,2},{2,0},{1,3},{3,1},{4,6},{6,4},{5,7},{7,5},{8,10},{10,8},{9,1... | collective-permute-start | bytes 393224 | tf_op jit(solution)/shard_map/ppermute | solution.py:25

commit v6 on v5

--- a/solution.py
+++ b/solution.py
@@ -47,9 +47,8 @@
             blocks, (here + steps) % count, axis=0, keepdims=False
         )
 
-    return [block(0)] + [
-        shifted(block(steps), axis, steps) for steps in range(1, count)
-    ]
+    order = sorted(range(1, count), key=lambda steps: -min(steps, count - steps))
+    return [block(0)] + [shifted(block(steps), axis, steps) for steps in order]
 
 
 def copies_kernel(value_ref, copies_ref, sems):

time: 126 us -> 123 us (0.976)
  blocking collectives: 29.9 us -> 26.9 us
    all_to_all x2, blocking collectives: 29.9 us -> 26.9 us  [exchange(): return lax.all_to_all(value, axis, split_axis=0, concat_axis=0, tiled=True)]
    all_to_all x4, waiting for transfers between devices: 14.2 us -> 15.8 us  [exchange(): return lax.all_to_all(value, axis, split_axis=0, concat_axis=0, tiled=True)]
  transfers between devices with their start and end apart: 11 -> 11, of which waited for: 6 -> 5; matrix products, arithmetic and copies ran while one was open for 5% -> 5% of each run, Pallas kernels for 3% -> 3%
where the time goes in v6:
time: 123 us; the launch traced here: 121 us
  starting transfers between devices  54.5 us (44%)
  blocking collectives  26.9 us (22%)
  waiting for transfers between devices  25 us (20%)
  other arithmetic  5.76 us (5%)
  Pallas kernels  3.98 us (3%)
  local copies, waits for them, and re-layouts  3.36 us (3%)
  matrix products  1.45 us (1%)
    all_to_all x4, starting transfers between devices, exchange(): return lax.all_to_all(value, axis, split_axis=0, concat_axis=0, tiled=True)  28.2 us
    all_to_all x2, blocking collectives, exchange(): return lax.all_to_all(value, axis, split_axis=0, concat_axis=0, tiled=True)  26.9 us
    ppermute x7, starting transfers between devices, shifted(): return lax.ppermute(value, axis, pairs)  26.4 us
    all_to_all x4, waiting for transfers between devices, exchange(): return lax.all_to_all(value, axis, split_axis=0, concat_axis=0, tiled=True)  15.8 us
    ppermute x7, waiting for transfers between devices, shifted(): return lax.ppermute(value, axis, pairs)  9.22 us
    pallas_call x1, Pallas kernels, turned_dot(): pl.pallas_call(turned_dot_kernel, out_shape=jax.ShapeDtypeStruct((rows, u...  3.21 us
  transfers between devices with their start and end apart: 11, of which 5 were waited for; matrix products, arithmetic and copies ran while one was open for 5% of the time, Pallas kernels for 3%

profile of v6, /device:TPU:6, one launch (start us, length us, event | category | flops | bytes accessed | tf_op | source)
XLA Modules:
  0.0 121.3 jit_solution(14029219074412583559)
XLA Ops:
  0.0 0.0 copy-start
  0.0 1.6 %broadcast_in_dim.17 = bf16[8,32,512]{2,1,0:T(8,128)(2,1)} broadcast(bf16[32,512]{1,0:T(8,128)(2,1)} %bitcast.44), dimensions={1,2} | broadcast | bytes 294912 | tf_op jit(solution)/shard_map/broadcast_in_dim | solution.py:19
  1.6 10.3 %all-to-all-start = ((bf16[8,32,512]{2,1,0:T(8,128)(2,1)}), bf16[8,32,512]{2,1,0:T(8,128)(2,1)S(1)}, u32[]{:S(2)}, u32[]{:S(2)}) async-start(bf16[8,32,512]{2,1,0:T(8,128)(2,1)} %broadcast_in_dim.17), calls=%async_computation | async-start | bytes 524288 | tf_op jit(solution)/shard_map/all_to_all | solution.py:15
  11.9 6.9 %collective-permute-start = (bf16[2,8192]{1,0:T(2,128)(2,1)}, bf16[2,8192]{1,0:T(2,128)(2,1)}, u32[]{:S(2)}, u32[]{:S(2)}) collective-permute-start(bf16[2,8192]{1,0:T(2,128)(2,1)} %bitcast.46), channel_id=1, source_target_pairs={{0,384},{128,0},{256,128},{384,256},{1,385},{129,1},{257,129},{385... | collective-permute-start | bytes 98312 | tf_op jit(solution)/shard_map/ppermute | solution.py:25
  18.9 4.9 %all-to-all-done = bf16[8,32,512]{2,1,0:T(8,128)(2,1)S(1)} async-done(((bf16[8,32,512]{2,1,0:T(8,128)(2,1)}), bf16[8,32,512]{2,1,0:T(8,128)(2,1)S(1)}, u32[]{:S(2)}, u32[]{:S(2)}) %all-to-all-start) | async-done | bytes 262176 | tf_op jit(solution)/shard_map/all_to_all | solution.py:15
  23.8 0.0 copy-done
  23.8 0.7 convolution_convert_fusion
  24.5 0.0 collective-permute-done
  24.6 7.8 %all-to-all-start.1 = ((bf16[16,2,512]{2,1,0:T(2,128)(2,1)}), bf16[16,2,512]{2,1,0:T(2,128)(2,1)S(1)}, u32[]{:S(2)}, u32[]{:S(2)}) async-start(bf16[16,2,512]{2,1,0:T(2,128)(2,1)} %bitcast.5), calls=%async_computation.1 | async-start | bytes 65536 | tf_op jit(solution)/shard_map/all_to_all | solution.py:15
  32.4 0.9 dynamic-slice_bitcast_fusion.2
  33.3 3.4 %collective-permute-start.1 = (bf16[64,2048]{1,0:T(8,128)(2,1)}, bf16[64,2048]{1,0:T(8,128)(2,1)}, u32[]{:S(2)}, u32[]{:S(2)}) collective-permute-start(bf16[64,2048]{1,0:T(8,128)(2,1)} %get-tuple-element.23), channel_id=1, source_target_pairs={{0,8},{4,12},{8,0},{12,4},{1,9},{5,13},{9,1},{13,5},{2,10},{6,14},... | collective-permute-start | bytes 786440 | tf_op jit(solution)/shard_map/ppermute | solution.py:25
  36.7 4.0 %collective-permute-start.2 = (bf16[64,2048]{1,0:T(8,128)(2,1)}, bf16[64,2048]{1,0:T(8,128)(2,1)}, u32[]{:S(2)}, u32[]{:S(2)}) collective-permute-start(bf16[64,2048]{1,0:T(8,128)(2,1)} %get-tuple-element.25), channel_id=1, source_target_pairs={{0,4},{4,8},{8,12},{12,0},{1,5},{5,9},{9,13},{13,1},{2,6},{6,10},{... | collective-permute-start | bytes 786440 | tf_op jit(solution)/shard_map/ppermute | solution.py:25
  40.7 1.9 %collective-permute-start.3 = (bf16[64,2048]{1,0:T(8,128)(2,1)}, bf16[64,2048]{1,0:T(8,128)(2,1)}, u32[]{:S(2)}, u32[]{:S(2)}) collective-permute-start(bf16[64,2048]{1,0:T(8,128)(2,1)} %get-tuple-element.24), channel_id=1, source_target_pairs={{0,12},{4,0},{8,4},{12,8},{1,13},{5,1},{9,5},{13,9},{2,14},{6,2},{... | collective-permute-start | bytes 786440 | tf_op jit(solution)/shard_map/ppermute | solution.py:25
  42.6 0.0 all-to-all-done.1
  42.6 0.8 shard_map.46
  43.4 3.4 %all-to-all-start.2 = ((bf16[8,32,512]{2,1,0:T(8,128)(2,1)}), bf16[8,32,512]{2,1,0:T(8,128)(2,1)S(1)}, u32[]{:S(2)}, u32[]{:S(2)}) async-start(bf16[8,32,512]{2,1,0:T(8,128)(2,1)} %shard_map.46), calls=%async_computation.2 | async-start | bytes 524288 | tf_op jit(solution)/shard_map/all_to_all | solution.py:15
  46.9 0.0 collective-permute-done.1
  46.9 0.0 collective-permute-done.2
  46.9 3.6 %collective-permute-done.3 = bf16[64,2048]{1,0:T(8,128)(2,1)} collective-permute-done((bf16[64,2048]{1,0:T(8,128)(2,1)}, bf16[64,2048]{1,0:T(8,128)(2,1)}, u32[]{:S(2)}, u32[]{:S(2)}) %collective-permute-start.3) | collective-permute-done | bytes 262176 | tf_op jit(solution)/shard_map/ppermute | solution.py:25
  50.5 1.2 %fusion.8 = bf16[64,2048]{1,0:T(8,128)(2,1)S(1)} fusion(bf16[64,2048]{1,0:T(8,128)(2,1)} %collective-permute-done.3, bf16[64,2048]{1,0:T(8,128)(2,1)} %collective-permute-done.2, bf16[64,2048]{1,0:T(8,128)(2,1)} %collective-permute-done.1, bf16[4,64,2048]{2,1,0:T(8,128)(2,1)S(1)} %bitcast.39, s32[]{:T(128)S(6)} %select_n.48), kind=kLoop, calls=%fused_computation.8 | loop fusion | flops 1048576 | bytes 1310724 | tf_op jit(solution)/shard_map/convert_element_type | solution.py:150
  51.7 0.7 dynamic-slice_bitcast_fusion.3
  52.4 3.4 %collective-permute-start.4 = (bf16[32,2048]{1,0:T(8,128)(2,1)S(1)}, bf16[32,2048]{1,0:T(8,128)(2,1)}, u32[]{:S(2)}, u32[]{:S(2)}) collective-permute-start(bf16[32,2048]{1,0:T(8,128)(2,1)S(1)} %get-tuple-element.26), channel_id=1, source_target_pairs={{0,1},{1,0},{2,3},{3,2},{4,5},{5,4},{6,7},{7,6},{8,9},{9,8},{10,11... | collective-permute-start | bytes 393224 | tf_op jit(solution)/shard_map/ppermute | solution.py:25
  55.8 1.9 %all-to-all-done.2 = bf16[8,32,512]{2,1,0:T(8,128)(2,1)S(1)} async-done(((bf16[8,32,512]{2,1,0:T(8,128)(2,1)}), bf16[8,32,512]{2,1,0:T(8,128)(2,1)S(1)}, u32[]{:S(2)}, u32[]{:S(2)}) %all-to-all-start.2) | async-done | bytes 262176 | tf_op jit(solution)/shard_map/all_to_all | solution.py:15
  57.7 3.2 %shard_map.47 = bf16[256,2048]{1,0:T(8,128)(2,1)} custom-call(bf16[256,512]{1,0:T(8,128)(2,1)S(1)} %bitcast.37, bf16[2048,512]{1,0:T(8,128)(2,1)} %bitcast.45), custom_call_target="tpu_custom_call" | custom-call | flops 20000000000 | bytes 1048576 | tf_op jit(solution)/shard_map/pallas_call | solution.py:111
  60.9 0.0 copy-start.1
  60.9 0.0 collective-permute-done.4
  60.9 6.6 %all-to-all-start.3 = ((bf16[8,32,2048]{2,1,0:T(8,128)(2,1)}), bf16[8,32,2048]{2,1,0:T(8,128)(2,1)S(1)}, u32[]{:S(2)}, u32[]{:S(2)}) async-start(bf16[8,32,2048]{2,1,0:T(8,128)(2,1)} %bitcast.16), calls=%async_computation.3 | async-start | bytes 2097152 | tf_op jit(solution)/shard_map/all_to_all | solution.py:15
  67.5 0.0 copy-done.1
  67.5 0.9 add_convert_fusion
  68.4 0.0 copy-start.2
  68.4 4.3 %collective-permute-start.5 = (bf16[32,2048]{1,0:T(8,128)(2,1)S(1)}, bf16[32,2048]{1,0:T(8,128)(2,1)}, u32[]{:S(2)}, u32[]{:S(2)}) collective-permute-start(bf16[32,2048]{1,0:T(8,128)(2,1)S(1)} %add_convert_fusion), channel_id=1, source_target_pairs={{0,2},{2,0},{1,3},{3,1},{4,6},{6,4},{5,7},{7,5},{8,10},{10,8},{9,1... | collective-permute-start | bytes 393224 | tf_op jit(solution)/shard_map/ppermute | solution.py:25
  72.7 8.9 %all-to-all-done.3 = bf16[8,32,2048]{2,1,0:T(8,128)(2,1)S(1)} async-done(((bf16[8,32,2048]{2,1,0:T(8,128)(2,1)}), bf16[8,32,2048]{2,1,0:T(8,128)(2,1)S(1)}, u32[]{:S(2)}, u32[]{:S(2)}) %all-to-all-start.3) | async-done | bytes 1048608 | tf_op jit(solution)/shard_map/all_to_all | solution.py:15
  81.7 0.8 reduce_sum.21
  82.5 0.0 collective-permute-done.5
  82.5 0.0 copy-done.2
  82.5 2.6 %collective-permute-start.6 = (bf16[32,2048]{1,0:T(8,128)(2,1)}, bf16[32,2048]{1,0:T(8,128)(2,1)S(1)}, u32[]{:S(2)}, u32[]{:S(2)}) collective-permute-start(bf16[32,2048]{1,0:T(8,128)(2,1)} %reduce_sum.21), channel_id=1, source_target_pairs={{0,2},{2,0},{1,3},{3,1},{4,6},{6,4},{5,7},{7,5},{8,10},{10,8},{9,1... | collective-permute-start | bytes 393224 | tf_op jit(solution)/shard_map/ppermute | solution.py:25
  85.1 1.2 fusion.13
  86.2 5.6 %collective-permute-done.6 = bf16[32,2048]{1,0:T(8,128)(2,1)S(1)} collective-permute-done((bf16[32,2048]{1,0:T(8,128)(2,1)}, bf16[32,2048]{1,0:T(8,128)(2,1)S(1)}, u32[]{:S(2)}, u32[]{:S(2)}) %collective-permute-start.6) | collective-permute-done | bytes 131104 | tf_op jit(solution)/shard_map/ppermute | solution.py:25
  91.8 1.0 multiply_convert_fusion
  92.8 0.1 broadcast_in_dim.18
  92.9 13.4 %all_to_all.30 = bf16[8,32,2048]{2,1,0:T(8,128)(2,1)S(1)} all-to-all(bf16[8,32,2048]{2,1,0:T(8,128)(2,1)S(1)} %broadcast_in_dim.18), channel_id=1, replica_groups=mesh['section'=4,'dp'=8,'tx'=4,'ty1'=2,'ty0'=2] {'tx','ty0'}, dimensions={0} | all-to-all | bytes 2097152 | tf_op jit(solution)/shard_map/all_to_all | solution.py:15
  106.3 0.7 fusion.3
  107.1 13.5 %all_to_all.31 = bf16[8,32,512]{2,1,0:T(8,128)(2,1)S(1)} all-to-all(bf16[8,32,512]{2,1,0:T(8,128)(2,1)S(1)} %bitcast.43), channel_id=1, replica_groups=mesh['section'=4,'dp'=8,'tx'=4,'ty1'=2,'ty0'=2] {'dp'}, dimensions={0} | all-to-all | bytes 524288 | tf_op jit(solution)/shard_map/all_to_all | solution.py:15
  120.6 0.6 fusion.14
  (2 shorter events, 0.1 us)
Async XLA Ops:
  0.0 23.8 %copy-start = (bf16[1,512,2048]{2,1,0:T(8,128)(2,1)S(1)}, bf16[1,512,2048]{2,1,0:T(8,128)(2,1)}, u32[]{:S(2)}) copy-start(bf16[1,512,2048]{2,1,0:T(8,128)(2,1)} %param.5) | copy-start | bytes 6291460
  1.6 22.2 %all-to-all-start = ((bf16[8,32,512]{2,1,0:T(8,128)(2,1)}), bf16[8,32,512]{2,1,0:T(8,128)(2,1)S(1)}, u32[]{:S(2)}, u32[]{:S(2)}) async-start(bf16[8,32,512]{2,1,0:T(8,128)(2,1)} %broadcast_in_dim.17), calls=%async_computation | async-start | bytes 524288 | tf_op jit(solution)/shard_map/all_to_all | solution.py:15
  11.9 12.6 %collective-permute-start = (bf16[2,8192]{1,0:T(2,128)(2,1)}, bf16[2,8192]{1,0:T(2,128)(2,1)}, u32[]{:S(2)}, u32[]{:S(2)}) collective-permute-start(bf16[2,8192]{1,0:T(2,128)(2,1)} %bitcast.46), channel_id=1, source_target_pairs={{0,384},{128,0},{256,128},{384,256},{1,385},{129,1},{257,129},{385... | collective-permute-start | bytes 98312 | tf_op jit(solution)/shard_map/ppermute | solution.py:25
  24.6 18.1 %all-to-all-start.1 = ((bf16[16,2,512]{2,1,0:T(2,128)(2,1)}), bf16[16,2,512]{2,1,0:T(2,128)(2,1)S(1)}, u32[]{:S(2)}, u32[]{:S(2)}) async-start(bf16[16,2,512]{2,1,0:T(2,128)(2,1)} %bitcast.5), calls=%async_computation.1 | async-start | bytes 65536 | tf_op jit(solution)/shard_map/all_to_all | solution.py:15
  33.3 13.5 %collective-permute-start.1 = (bf16[64,2048]{1,0:T(8,128)(2,1)}, bf16[64,2048]{1,0:T(8,128)(2,1)}, u32[]{:S(2)}, u32[]{:S(2)}) collective-permute-start(bf16[64,2048]{1,0:T(8,128)(2,1)} %get-tuple-element.23), channel_id=1, source_target_pairs={{0,8},{4,12},{8,0},{12,4},{1,9},{5,13},{9,1},{13,5},{2,10},{6,14},... | collective-permute-start | bytes 786440 | tf_op jit(solution)/shard_map/ppermute | solution.py:25
  36.7 10.2 %collective-permute-start.2 = (bf16[64,2048]{1,0:T(8,128)(2,1)}, bf16[64,2048]{1,0:T(8,128)(2,1)}, u32[]{:S(2)}, u32[]{:S(2)}) collective-permute-start(bf16[64,2048]{1,0:T(8,128)(2,1)} %get-tuple-element.25), channel_id=1, source_target_pairs={{0,4},{4,8},{8,12},{12,0},{1,5},{5,9},{9,13},{13,1},{2,6},{6,10},{... | collective-permute-start | bytes 786440 | tf_op jit(solution)/shard_map/ppermute | solution.py:25
  40.7 9.8 %collective-permute-start.3 = (bf16[64,2048]{1,0:T(8,128)(2,1)}, bf16[64,2048]{1,0:T(8,128)(2,1)}, u32[]{:S(2)}, u32[]{:S(2)}) collective-permute-start(bf16[64,2048]{1,0:T(8,128)(2,1)} %get-tuple-element.24), channel_id=1, source_target_pairs={{0,12},{4,0},{8,4},{12,8},{1,13},{5,1},{9,5},{13,9},{2,14},{6,2},{... | collective-permute-start | bytes 786440 | tf_op jit(solution)/shard_map/ppermute | solution.py:25
  43.4 14.2 %all-to-all-start.2 = ((bf16[8,32,512]{2,1,0:T(8,128)(2,1)}), bf16[8,32,512]{2,1,0:T(8,128)(2,1)S(1)}, u32[]{:S(2)}, u32[]{:S(2)}) async-start(bf16[8,32,512]{2,1,0:T(8,128)(2,1)} %shard_map.46), calls=%async_computation.2 | async-start | bytes 524288 | tf_op jit(solution)/shard_map/all_to_all | solution.py:15
  52.4 8.5 %collective-permute-start.4 = (bf16[32,2048]{1,0:T(8,128)(2,1)S(1)}, bf16[32,2048]{1,0:T(8,128)(2,1)}, u32[]{:S(2)}, u32[]{:S(2)}) collective-permute-start(bf16[32,2048]{1,0:T(8,128)(2,1)S(1)} %get-tuple-element.26), channel_id=1, source_target_pairs={{0,1},{1,0},{2,3},{3,2},{4,5},{5,4},{6,7},{7,6},{8,9},{9,8},{10,11... | collective-permute-start | bytes 393224 | tf_op jit(solution)/shard_map/ppermute | solution.py:25
  60.9 6.6 %copy-start.1 = (bf16[32,2048]{1,0:T(8,128)(2,1)S(1)}, bf16[32,2048]{1,0:T(8,128)(2,1)}, u32[]{:S(2)}) copy-start(bf16[32,2048]{1,0:T(8,128)(2,1)} %get-tuple-element.17) | copy-start | bytes 393220
  60.9 20.8 %all-to-all-start.3 = ((bf16[8,32,2048]{2,1,0:T(8,128)(2,1)}), bf16[8,32,2048]{2,1,0:T(8,128)(2,1)S(1)}, u32[]{:S(2)}, u32[]{:S(2)}) async-start(bf16[8,32,2048]{2,1,0:T(8,128)(2,1)} %bitcast.16), calls=%async_computation.3 | async-start | bytes 2097152 | tf_op jit(solution)/shard_map/all_to_all | solution.py:15
  68.4 14.1 %copy-start.2 = (bf16[32,2048]{1,0:T(8,128)(2,1)}, bf16[32,2048]{1,0:T(8,128)(2,1)S(1)}, u32[]{:S(2)}) copy-start(bf16[32,2048]{1,0:T(8,128)(2,1)S(1)} %add_convert_fusion) | copy-start | bytes 393220
  68.4 14.0 %collective-permute-start.5 = (bf16[32,2048]{1,0:T(8,128)(2,1)S(1)}, bf16[32,2048]{1,0:T(8,128)(2,1)}, u32[]{:S(2)}, u32[]{:S(2)}) collective-permute-start(bf16[32,2048]{1,0:T(8,128)(2,1)S(1)} %add_convert_fusion), channel_id=1, source_target_pairs={{0,2},{2,0},{1,3},{3,1},{4,6},{6,4},{5,7},{7,5},{8,10},{10,8},{9,1... | collective-permute-start | bytes 393224 | tf_op jit(solution)/shard_map/ppermute | solution.py:25
  82.5 9.4 %collective-permute-start.6 = (bf16[32,2048]{1,0:T(8,128)(2,1)}, bf16[32,2048]{1,0:T(8,128)(2,1)S(1)}, u32[]{:S(2)}, u32[]{:S(2)}) collective-permute-start(bf16[32,2048]{1,0:T(8,128)(2,1)} %reduce_sum.21), channel_id=1, source_target_pairs={{0,2},{2,0},{1,3},{3,1},{4,6},{6,4},{5,7},{7,5},{8,10},{10,8},{9,1... | collective-permute-start | bytes 393224 | tf_op jit(solution)/shard_map/ppermute | solution.py:25

commit v7 on v6

--- a/solution.py
+++ b/solution.py
@@ -6,7 +6,7 @@
 from jax.sharding import Mesh
 from jax.sharding import PartitionSpec as P
 
-LONG = pl.CostEstimate(flops=2 * 10**10, bytes_accessed=2**20, transcendentals=0)
+LONG = pl.CostEstimate(flops=2 * 10**11, bytes_accessed=2**20, transcendentals=0)
 TENSOR = ("tx", "ty1", "ty0")
 NEAR = ("tx", "ty0")
 
@@ -47,7 +47,7 @@
             blocks, (here + steps) % count, axis=0, keepdims=False
         )
 
-    order = sorted(range(1, count), key=lambda steps: -min(steps, count - steps))
+    order = sorted(range(1, count), key=lambda steps: (-min(steps, count - steps), -steps))
     return [block(0)] + [shifted(block(steps), axis, steps) for steps in order]
 
 

time: 123 us -> 122 us (level)
  other arithmetic: 5.76 us -> 3.31 us
    ppermute x7, waiting for transfers between devices: 9.22 us -> 6.62 us  [shifted(): return lax.ppermute(value, axis, pairs)]
    all_to_all x4, waiting for transfers between devices: 15.8 us -> 18.4 us  [exchange(): return lax.all_to_all(value, axis, split_axis=0, concat_axis=0, tiled=True)]
    ppermute x7, starting transfers between devices: 26.4 us -> 27.6 us  [shifted(): return lax.ppermute(value, axis, pairs)]
  transfers between devices with their start and end apart: 11 -> 11, of which waited for: 5 -> 5; matrix products, arithmetic and copies ran while one was open for 5% -> 4% of each run, Pallas kernels for 3% -> 3%
where the time goes in v7:
time: 122 us; the launch traced here: 120 us
  starting transfers between devices  54.7 us (45%)
  blocking collectives  27.8 us (23%)
  waiting for transfers between devices  25 us (20%)
  Pallas kernels  4 us (3%)
  local copies, waits for them, and re-layouts  3.44 us (3%)
  other arithmetic  3.31 us (3%)
  matrix products  1.46 us (1%)
    all_to_all x2, blocking collectives, exchange(): return lax.all_to_all(value, axis, split_axis=0, concat_axis=0, tiled=True)  27.8 us
    ppermute x7, starting transfers between devices, shifted(): return lax.ppermute(value, axis, pairs)  27.6 us
    all_to_all x4, starting transfers between devices, exchange(): return lax.all_to_all(value, axis, split_axis=0, concat_axis=0, tiled=True)  27.1 us
    all_to_all x4, waiting for transfers between devices, exchange(): return lax.all_to_all(value, axis, split_axis=0, concat_axis=0, tiled=True)  18.4 us
    ppermute x7, waiting for transfers between devices, shifted(): return lax.ppermute(value, axis, pairs)  6.62 us
    pallas_call x1, Pallas kernels, turned_dot(): pl.pallas_call(turned_dot_kernel, out_shape=jax.ShapeDtypeStruct((rows, u...  3.2 us
  transfers between devices with their start and end apart: 11, of which 5 were waited for; matrix products, arithmetic and copies ran while one was open for 4% of the time, Pallas kernels for 3%

profile of v7, /device:TPU:6, one launch (start us, length us, event | category | flops | bytes accessed | tf_op | source)
XLA Modules:
  0.0 120.0 jit_solution(2048394507352431716)
XLA Ops:
  0.0 0.0 copy-start
  0.0 1.6 %broadcast_in_dim.17 = bf16[8,32,512]{2,1,0:T(8,128)(2,1)} broadcast(bf16[32,512]{1,0:T(8,128)(2,1)} %bitcast.44), dimensions={1,2} | broadcast | bytes 294912 | tf_op jit(solution)/shard_map/broadcast_in_dim | solution.py:19
  1.6 10.3 %all-to-all-start = ((bf16[8,32,512]{2,1,0:T(8,128)(2,1)}), bf16[8,32,512]{2,1,0:T(8,128)(2,1)S(1)}, u32[]{:S(2)}, u32[]{:S(2)}) async-start(bf16[8,32,512]{2,1,0:T(8,128)(2,1)} %broadcast_in_dim.17), calls=%async_computation | async-start | bytes 524288 | tf_op jit(solution)/shard_map/all_to_all | solution.py:15
  11.9 6.9 %collective-permute-start = (bf16[2,8192]{1,0:T(2,128)(2,1)}, bf16[2,8192]{1,0:T(2,128)(2,1)}, u32[]{:S(2)}, u32[]{:S(2)}) collective-permute-start(bf16[2,8192]{1,0:T(2,128)(2,1)} %bitcast.46), channel_id=1, source_target_pairs={{0,384},{128,0},{256,128},{384,256},{1,385},{129,1},{257,129},{385... | collective-permute-start | bytes 98312 | tf_op jit(solution)/shard_map/ppermute | solution.py:25
  18.9 4.9 %all-to-all-done = bf16[8,32,512]{2,1,0:T(8,128)(2,1)S(1)} async-done(((bf16[8,32,512]{2,1,0:T(8,128)(2,1)}), bf16[8,32,512]{2,1,0:T(8,128)(2,1)S(1)}, u32[]{:S(2)}, u32[]{:S(2)}) %all-to-all-start) | async-done | bytes 262176 | tf_op jit(solution)/shard_map/all_to_all | solution.py:15
  23.8 0.0 copy-done
  23.8 0.7 convolution_convert_fusion
  24.5 0.0 copy-start.3
  24.6 0.0 collective-permute-done
  24.6 7.8 %all-to-all-start.1 = ((bf16[16,2,512]{2,1,0:T(2,128)(2,1)}), bf16[16,2,512]{2,1,0:T(2,128)(2,1)S(1)}, u32[]{:S(2)}, u32[]{:S(2)}) async-start(bf16[16,2,512]{2,1,0:T(2,128)(2,1)} %bitcast.5), calls=%async_computation.1 | async-start | bytes 65536 | tf_op jit(solution)/shard_map/all_to_all | solution.py:15
  32.4 0.9 dynamic-slice_bitcast_fusion.2
  33.3 3.4 %collective-permute-start.1 = (bf16[64,2048]{1,0:T(8,128)(2,1)}, bf16[64,2048]{1,0:T(8,128)(2,1)}, u32[]{:S(2)}, u32[]{:S(2)}) collective-permute-start(bf16[64,2048]{1,0:T(8,128)(2,1)} %get-tuple-element.23), channel_id=1, source_target_pairs={{0,8},{4,12},{8,0},{12,4},{1,9},{5,13},{9,1},{13,5},{2,10},{6,14},... | collective-permute-start | bytes 786440 | tf_op jit(solution)/shard_map/ppermute | solution.py:25
  36.7 1.9 %collective-permute-start.2 = (bf16[64,2048]{1,0:T(8,128)(2,1)}, bf16[64,2048]{1,0:T(8,128)(2,1)}, u32[]{:S(2)}, u32[]{:S(2)}) collective-permute-start(bf16[64,2048]{1,0:T(8,128)(2,1)} %get-tuple-element.25), channel_id=1, source_target_pairs={{0,12},{4,0},{8,4},{12,8},{1,13},{5,1},{9,5},{13,9},{2,14},{6,2},{... | collective-permute-start | bytes 786440 | tf_op jit(solution)/shard_map/ppermute | solution.py:25
  38.6 5.1 %collective-permute-start.3 = (bf16[64,2048]{1,0:T(8,128)(2,1)}, bf16[64,2048]{1,0:T(8,128)(2,1)}, u32[]{:S(2)}, u32[]{:S(2)}) collective-permute-start(bf16[64,2048]{1,0:T(8,128)(2,1)} %get-tuple-element.24), channel_id=1, source_target_pairs={{0,4},{4,8},{8,12},{12,0},{1,5},{5,9},{9,13},{13,1},{2,6},{6,10},{... | collective-permute-start | bytes 786440 | tf_op jit(solution)/shard_map/ppermute | solution.py:25
  43.8 0.0 copy-done.3
  43.8 0.0 all-to-all-done.1
  43.8 0.0 copy-start.1
  43.8 0.8 shard_map.46
  44.6 0.0 copy-done.1
  44.7 3.4 %all-to-all-start.2 = ((bf16[8,32,512]{2,1,0:T(8,128)(2,1)}), bf16[8,32,512]{2,1,0:T(8,128)(2,1)S(1)}, u32[]{:S(2)}, u32[]{:S(2)}) async-start(bf16[8,32,512]{2,1,0:T(8,128)(2,1)} %shard_map.46), calls=%async_computation.2 | async-start | bytes 524288 | tf_op jit(solution)/shard_map/all_to_all | solution.py:15
  48.1 0.0 collective-permute-done.1
  48.1 0.4 collective-permute-done.2
  48.5 0.0 collective-permute-done.3
  48.5 1.3 %fusion.8 = bf16[64,2048]{1,0:T(8,128)(2,1)S(1)} fusion(bf16[64,2048]{1,0:T(8,128)(2,1)} %collective-permute-done.3, bf16[64,2048]{1,0:T(8,128)(2,1)} %collective-permute-done.2, bf16[64,2048]{1,0:T(8,128)(2,1)} %collective-permute-done.1, bf16[4,64,2048]{2,1,0:T(8,128)(2,1)} %bitcast.39, s32[]{:T(128)S(6)} %select_n.48), kind=kLoop, calls=%fused_computation.8 | loop fusion | flops 1048576 | bytes 1310724 | tf_op jit(solution)/shard_map/convert_element_type | solution.py:150
  49.8 0.7 dynamic-slice_bitcast_fusion.3
  50.5 3.3 %collective-permute-start.4 = (bf16[32,2048]{1,0:T(8,128)(2,1)}, bf16[32,2048]{1,0:T(8,128)(2,1)}, u32[]{:S(2)}, u32[]{:S(2)}) collective-permute-start(bf16[32,2048]{1,0:T(8,128)(2,1)} %get-tuple-element.26), channel_id=1, source_target_pairs={{0,1},{1,0},{2,3},{3,2},{4,5},{5,4},{6,7},{7,6},{8,9},{9,8},{10,11... | collective-permute-start | bytes 393224 | tf_op jit(solution)/shard_map/ppermute | solution.py:25
  53.8 4.8 %all-to-all-done.2 = bf16[8,32,512]{2,1,0:T(8,128)(2,1)S(1)} async-done(((bf16[8,32,512]{2,1,0:T(8,128)(2,1)}), bf16[8,32,512]{2,1,0:T(8,128)(2,1)S(1)}, u32[]{:S(2)}, u32[]{:S(2)}) %all-to-all-start.2) | async-done | bytes 262176 | tf_op jit(solution)/shard_map/all_to_all | solution.py:15
  58.6 3.2 %shard_map.47 = bf16[256,2048]{1,0:T(8,128)(2,1)} custom-call(bf16[256,512]{1,0:T(8,128)(2,1)S(1)} %bitcast.37, bf16[2048,512]{1,0:T(8,128)(2,1)} %bitcast.45), custom_call_target="tpu_custom_call" | custom-call | flops 199999995904 | bytes 1048576 | tf_op jit(solution)/shard_map/pallas_call | solution.py:111
  61.8 0.0 copy-start.4
  61.8 0.0 collective-permute-done.4
  61.8 5.5 %all-to-all-start.3 = ((bf16[8,32,2048]{2,1,0:T(8,128)(2,1)}), bf16[8,32,2048]{2,1,0:T(8,128)(2,1)S(1)}, u32[]{:S(2)}, u32[]{:S(2)}) async-start(bf16[8,32,2048]{2,1,0:T(8,128)(2,1)} %bitcast.16), calls=%async_computation.3 | async-start | bytes 2097152 | tf_op jit(solution)/shard_map/all_to_all | solution.py:15
  67.4 0.0 copy-done.4
  67.4 0.9 add_convert_fusion
  68.3 4.3 %collective-permute-start.5 = (bf16[32,2048]{1,0:T(8,128)(2,1)S(1)}, bf16[32,2048]{1,0:T(8,128)(2,1)S(1)}, u32[]{:S(2)}, u32[]{:S(2)}) collective-permute-start(bf16[32,2048]{1,0:T(8,128)(2,1)S(1)} %add_convert_fusion), channel_id=1, source_target_pairs={{0,2},{2,0},{1,3},{3,1},{4,6},{6,4},{5,7},{7,5},{8,10},{10,8},{9,1... | collective-permute-start | bytes 393224 | tf_op jit(solution)/shard_map/ppermute | solution.py:25
  72.6 8.7 %all-to-all-done.3 = bf16[8,32,2048]{2,1,0:T(8,128)(2,1)S(1)} async-done(((bf16[8,32,2048]{2,1,0:T(8,128)(2,1)}), bf16[8,32,2048]{2,1,0:T(8,128)(2,1)S(1)}, u32[]{:S(2)}, u32[]{:S(2)}) %all-to-all-start.3) | async-done | bytes 1048608 | tf_op jit(solution)/shard_map/all_to_all | solution.py:15
  81.3 0.1 reduce_sum.21
  81.4 0.0 collective-permute-done.5
  81.5 2.7 %collective-permute-start.6 = (bf16[32,2048]{1,0:T(8,128)(2,1)S(1)}, bf16[32,2048]{1,0:T(8,128)(2,1)S(1)}, u32[]{:S(2)}, u32[]{:S(2)}) collective-permute-start(bf16[32,2048]{1,0:T(8,128)(2,1)S(1)} %reduce_sum.21), channel_id=1, source_target_pairs={{0,2},{2,0},{1,3},{3,1},{4,6},{6,4},{5,7},{7,5},{8,10},{10,8},{9,1... | collective-permute-start | bytes 393224 | tf_op jit(solution)/shard_map/ppermute | solution.py:25
  84.2 0.2 fusion.13
  84.4 6.3 %collective-permute-done.6 = bf16[32,2048]{1,0:T(8,128)(2,1)S(1)} collective-permute-done((bf16[32,2048]{1,0:T(8,128)(2,1)S(1)}, bf16[32,2048]{1,0:T(8,128)(2,1)S(1)}, u32[]{:S(2)}, u32[]{:S(2)}) %collective-permute-start.6) | collective-permute-done | bytes 131104 | tf_op jit(solution)/shard_map/ppermute | solution.py:25
  90.7 0.1 broadcast_in_dim.18
  90.8 13.5 %all_to_all.30 = bf16[8,32,2048]{2,1,0:T(8,128)(2,1)S(1)} all-to-all(bf16[8,32,2048]{2,1,0:T(8,128)(2,1)S(1)} %broadcast_in_dim.18), channel_id=1, replica_groups=mesh['section'=4,'dp'=8,'tx'=4,'ty1'=2,'ty0'=2] {'tx','ty0'}, dimensions={0} | all-to-all | bytes 2097152 | tf_op jit(solution)/shard_map/all_to_all | solution.py:15
  104.3 0.0 copy-start.2
  104.3 0.7 fusion.3
  105.1 14.2 %all_to_all.31 = bf16[8,32,512]{2,1,0:T(8,128)(2,1)S(1)} all-to-all(bf16[8,32,512]{2,1,0:T(8,128)(2,1)S(1)} %bitcast.43), channel_id=1, replica_groups=mesh['section'=4,'dp'=8,'tx'=4,'ty1'=2,'ty0'=2] {'dp'}, dimensions={0} | all-to-all | bytes 524288 | tf_op jit(solution)/shard_map/all_to_all | solution.py:15
  119.4 0.0 copy-done.2
  119.4 0.6 fusion.14
  (3 shorter events, 0.1 us)
Async XLA Ops:
  0.0 23.8 %copy-start = (bf16[1,512,2048]{2,1,0:T(8,128)(2,1)S(1)}, bf16[1,512,2048]{2,1,0:T(8,128)(2,1)}, u32[]{:S(2)}) copy-start(bf16[1,512,2048]{2,1,0:T(8,128)(2,1)} %param.5) | copy-start | bytes 6291460
  1.6 22.2 %all-to-all-start = ((bf16[8,32,512]{2,1,0:T(8,128)(2,1)}), bf16[8,32,512]{2,1,0:T(8,128)(2,1)S(1)}, u32[]{:S(2)}, u32[]{:S(2)}) async-start(bf16[8,32,512]{2,1,0:T(8,128)(2,1)} %broadcast_in_dim.17), calls=%async_computation | async-start | bytes 524288 | tf_op jit(solution)/shard_map/all_to_all | solution.py:15
  11.9 12.6 %collective-permute-start = (bf16[2,8192]{1,0:T(2,128)(2,1)}, bf16[2,8192]{1,0:T(2,128)(2,1)}, u32[]{:S(2)}, u32[]{:S(2)}) collective-permute-start(bf16[2,8192]{1,0:T(2,128)(2,1)} %bitcast.46), channel_id=1, source_target_pairs={{0,384},{128,0},{256,128},{384,256},{1,385},{129,1},{257,129},{385... | collective-permute-start | bytes 98312 | tf_op jit(solution)/shard_map/ppermute | solution.py:25
  24.5 19.2 %copy-start.3 = (bf16[256,2048]{1,0:T(8,128)(2,1)}, bf16[256,2048]{1,0:T(8,128)(2,1)S(1)}, u32[]{:S(2)}) copy-start(bf16[256,2048]{1,0:T(8,128)(2,1)S(1)} %convolution_convert_fusion) | copy-start | bytes 3145732
  24.6 19.2 %all-to-all-start.1 = ((bf16[16,2,512]{2,1,0:T(2,128)(2,1)}), bf16[16,2,512]{2,1,0:T(2,128)(2,1)S(1)}, u32[]{:S(2)}, u32[]{:S(2)}) async-start(bf16[16,2,512]{2,1,0:T(2,128)(2,1)} %bitcast.5), calls=%async_computation.1 | async-start | bytes 65536 | tf_op jit(solution)/shard_map/all_to_all | solution.py:15
  33.3 14.7 %collective-permute-start.1 = (bf16[64,2048]{1,0:T(8,128)(2,1)}, bf16[64,2048]{1,0:T(8,128)(2,1)}, u32[]{:S(2)}, u32[]{:S(2)}) collective-permute-start(bf16[64,2048]{1,0:T(8,128)(2,1)} %get-tuple-element.23), channel_id=1, source_target_pairs={{0,8},{4,12},{8,0},{12,4},{1,9},{5,13},{9,1},{13,5},{2,10},{6,14},... | collective-permute-start | bytes 786440 | tf_op jit(solution)/shard_map/ppermute | solution.py:25
  36.7 11.7 %collective-permute-start.2 = (bf16[64,2048]{1,0:T(8,128)(2,1)}, bf16[64,2048]{1,0:T(8,128)(2,1)}, u32[]{:S(2)}, u32[]{:S(2)}) collective-permute-start(bf16[64,2048]{1,0:T(8,128)(2,1)} %get-tuple-element.25), channel_id=1, source_target_pairs={{0,12},{4,0},{8,4},{12,8},{1,13},{5,1},{9,5},{13,9},{2,14},{6,2},{... | collective-permute-start | bytes 786440 | tf_op jit(solution)/shard_map/ppermute | solution.py:25
  38.6 9.8 %collective-permute-start.3 = (bf16[64,2048]{1,0:T(8,128)(2,1)}, bf16[64,2048]{1,0:T(8,128)(2,1)}, u32[]{:S(2)}, u32[]{:S(2)}) collective-permute-start(bf16[64,2048]{1,0:T(8,128)(2,1)} %get-tuple-element.24), channel_id=1, source_target_pairs={{0,4},{4,8},{8,12},{12,0},{1,5},{5,9},{9,13},{13,1},{2,6},{6,10},{... | collective-permute-start | bytes 786440 | tf_op jit(solution)/shard_map/ppermute | solution.py:25
  43.8 0.8 copy-start.1
  44.7 14.0 %all-to-all-start.2 = ((bf16[8,32,512]{2,1,0:T(8,128)(2,1)}), bf16[8,32,512]{2,1,0:T(8,128)(2,1)S(1)}, u32[]{:S(2)}, u32[]{:S(2)}) async-start(bf16[8,32,512]{2,1,0:T(8,128)(2,1)} %shard_map.46), calls=%async_computation.2 | async-start | bytes 524288 | tf_op jit(solution)/shard_map/all_to_all | solution.py:15
  50.5 11.3 %collective-permute-start.4 = (bf16[32,2048]{1,0:T(8,128)(2,1)}, bf16[32,2048]{1,0:T(8,128)(2,1)}, u32[]{:S(2)}, u32[]{:S(2)}) collective-permute-start(bf16[32,2048]{1,0:T(8,128)(2,1)} %get-tuple-element.26), channel_id=1, source_target_pairs={{0,1},{1,0},{2,3},{3,2},{4,5},{5,4},{6,7},{7,6},{8,9},{9,8},{10,11... | collective-permute-start | bytes 393224 | tf_op jit(solution)/shard_map/ppermute | solution.py:25
  61.8 5.6 %copy-start.4 = (bf16[32,2048]{1,0:T(8,128)(2,1)S(1)}, bf16[32,2048]{1,0:T(8,128)(2,1)}, u32[]{:S(2)}) copy-start(bf16[32,2048]{1,0:T(8,128)(2,1)} %get-tuple-element.17) | copy-start | bytes 393220
  61.8 19.5 %all-to-all-start.3 = ((bf16[8,32,2048]{2,1,0:T(8,128)(2,1)}), bf16[8,32,2048]{2,1,0:T(8,128)(2,1)S(1)}, u32[]{:S(2)}, u32[]{:S(2)}) async-start(bf16[8,32,2048]{2,1,0:T(8,128)(2,1)} %bitcast.16), calls=%async_computation.3 | async-start | bytes 2097152 | tf_op jit(solution)/shard_map/all_to_all | solution.py:15
  68.3 13.1 %collective-permute-start.5 = (bf16[32,2048]{1,0:T(8,128)(2,1)S(1)}, bf16[32,2048]{1,0:T(8,128)(2,1)S(1)}, u32[]{:S(2)}, u32[]{:S(2)}) collective-permute-start(bf16[32,2048]{1,0:T(8,128)(2,1)S(1)} %add_convert_fusion), channel_id=1, source_target_pairs={{0,2},{2,0},{1,3},{3,1},{4,6},{6,4},{5,7},{7,5},{8,10},{10,8},{9,1... | collective-permute-start | bytes 393224 | tf_op jit(solution)/shard_map/ppermute | solution.py:25
  81.5 9.2 %collective-permute-start.6 = (bf16[32,2048]{1,0:T(8,128)(2,1)S(1)}, bf16[32,2048]{1,0:T(8,128)(2,1)S(1)}, u32[]{:S(2)}, u32[]{:S(2)}) collective-permute-start(bf16[32,2048]{1,0:T(8,128)(2,1)S(1)} %reduce_sum.21), channel_id=1, source_target_pairs={{0,2},{2,0},{1,3},{3,1},{4,6},{6,4},{5,7},{7,5},{8,10},{10,8},{9,1... | collective-permute-start | bytes 393224 | tf_op jit(solution)/shard_map/ppermute | solution.py:25
  104.3 15.0 %copy-start.2 = (bf16[32,512]{1,0:T(8,128)(2,1)S(1)}, bf16[32,512]{1,0:T(8,128)(2,1)}, u32[]{:S(2)}) copy-start(bf16[32,512]{1,0:T(8,128)(2,1)} %copy-done.1) | copy-start | bytes 98308

commit v8 on v7

--- a/solution.py
+++ b/solution.py
@@ -138,12 +138,12 @@
 
     moved = shifted(sent, "section", -1)
     all_tokens = exchange(copies(tokens_in, "dp"), "dp").reshape(-1, width)
+    all_tokens, moved = lax.optimization_barrier((all_tokens, moved))
     hidden_part = jnp.dot(
         all_tokens, up_block, preferred_element_type=jnp.float32
     ).astype(jnp.bfloat16)
     units = hidden_part.shape[1]
 
-    hidden_part, moved = lax.optimization_barrier((hidden_part, moved))
     moved = moved.reshape(-1, parts, width).transpose(1, 0, 2)
     local_grad = exchange(moved, TENSOR).reshape(rows, width)
     (local_grad,) = lax.optimization_barrier((local_grad,))

time: 122 us -> 124 us (1.016)
  waiting for transfers between devices: 25 us -> 26.5 us
    ppermute x7, waiting for transfers between devices: 6.62 us -> 8.51 us  [shifted(): return lax.ppermute(value, axis, pairs)]
  transfers between devices with their start and end apart: 11 -> 11, of which waited for: 5 -> 6; matrix products, arithmetic and copies ran while one was open for 4% -> 4% of each run, Pallas kernels for 3% -> 3%
where the time goes in v8:
time: 124 us; the launch traced here: 122 us
  starting transfers between devices  54.6 us (44%)
  blocking collectives  27.7 us (22%)
  waiting for transfers between devices  26.5 us (21%)
  local copies, waits for them, and re-layouts  4.41 us (4%)
  Pallas kernels  4 us (3%)
  other arithmetic  3.31 us (3%)
  matrix products  1.46 us (1%)
    all_to_all x2, blocking collectives, exchange(): return lax.all_to_all(value, axis, split_axis=0, concat_axis=0, tiled=True)  27.7 us
    ppermute x7, starting transfers between devices, shifted(): return lax.ppermute(value, axis, pairs)  27.5 us
    all_to_all x4, starting transfers between devices, exchange(): return lax.all_to_all(value, axis, split_axis=0, concat_axis=0, tiled=True)  27.1 us
    all_to_all x4, waiting for transfers between devices, exchange(): return lax.all_to_all(value, axis, split_axis=0, concat_axis=0, tiled=True)  18 us
    ppermute x7, waiting for transfers between devices, shifted(): return lax.ppermute(value, axis, pairs)  8.51 us
    pallas_call x1, Pallas kernels, turned_dot(): pl.pallas_call(turned_dot_kernel, out_shape=jax.ShapeDtypeStruct((rows, u...  3.2 us
  transfers between devices with their start and end apart: 11, of which 6 were waited for; matrix products, arithmetic and copies ran while one was open for 4% of the time, Pallas kernels for 3%

profile of v8, /device:TPU:6, one launch (start us, length us, event | category | flops | bytes accessed | tf_op | source)
XLA Modules:
  0.0 122.3 jit_solution(8422359626375942191)
XLA Ops:
  0.0 0.0 copy-start
  0.0 1.6 %broadcast_in_dim.17 = bf16[8,32,512]{2,1,0:T(8,128)(2,1)} broadcast(bf16[32,512]{1,0:T(8,128)(2,1)} %bitcast.44), dimensions={1,2} | broadcast | bytes 294912 | tf_op jit(solution)/shard_map/broadcast_in_dim | solution.py:19
  1.6 10.3 %all-to-all-start = ((bf16[8,32,512]{2,1,0:T(8,128)(2,1)}), bf16[8,32,512]{2,1,0:T(8,128)(2,1)S(1)}, u32[]{:S(2)}, u32[]{:S(2)}) async-start(bf16[8,32,512]{2,1,0:T(8,128)(2,1)} %broadcast_in_dim.17), calls=%async_computation | async-start | bytes 524288 | tf_op jit(solution)/shard_map/all_to_all | solution.py:15
  11.9 6.9 %collective-permute-start = (bf16[2,8192]{1,0:T(2,128)(2,1)}, bf16[2,8192]{1,0:T(2,128)(2,1)}, u32[]{:S(2)}, u32[]{:S(2)}) collective-permute-start(bf16[2,8192]{1,0:T(2,128)(2,1)} %bitcast.46), channel_id=1, source_target_pairs={{0,384},{128,0},{256,128},{384,256},{1,385},{129,1},{257,129},{385... | collective-permute-start | bytes 98312 | tf_op jit(solution)/shard_map/ppermute | solution.py:25
  18.9 1.8 %collective-permute-done = bf16[2,8192]{1,0:T(2,128)(2,1)} collective-permute-done((bf16[2,8192]{1,0:T(2,128)(2,1)}, bf16[2,8192]{1,0:T(2,128)(2,1)}, u32[]{:S(2)}, u32[]{:S(2)}) %collective-permute-start) | collective-permute-done | bytes 32800 | tf_op jit(solution)/shard_map/ppermute | solution.py:25
  20.7 3.1 %all-to-all-done = bf16[8,32,512]{2,1,0:T(8,128)(2,1)S(1)} async-done(((bf16[8,32,512]{2,1,0:T(8,128)(2,1)}), bf16[8,32,512]{2,1,0:T(8,128)(2,1)S(1)}, u32[]{:S(2)}, u32[]{:S(2)}) %all-to-all-start) | async-done | bytes 262176 | tf_op jit(solution)/shard_map/all_to_all | solution.py:15
  23.8 7.8 %all-to-all-start.1 = ((bf16[16,2,512]{2,1,0:T(2,128)(2,1)}), bf16[16,2,512]{2,1,0:T(2,128)(2,1)S(1)}, u32[]{:S(2)}, u32[]{:S(2)}) async-start(bf16[16,2,512]{2,1,0:T(2,128)(2,1)} %bitcast.4), calls=%async_computation.1 | async-start | bytes 65536 | tf_op jit(solution)/shard_map/all_to_all | solution.py:15
  31.7 0.0 copy-done
  31.7 0.7 convolution_convert_fusion
  32.4 0.0 copy-start.3
  32.4 1.0 copy-done.3
  33.4 0.9 dynamic-slice_bitcast_fusion.2
  34.3 3.4 %collective-permute-start.1 = (bf16[64,2048]{1,0:T(8,128)(2,1)}, bf16[64,2048]{1,0:T(8,128)(2,1)}, u32[]{:S(2)}, u32[]{:S(2)}) collective-permute-start(bf16[64,2048]{1,0:T(8,128)(2,1)} %get-tuple-element.23), channel_id=1, source_target_pairs={{0,8},{4,12},{8,0},{12,4},{1,9},{5,13},{9,1},{13,5},{2,10},{6,14},... | collective-permute-start | bytes 786440 | tf_op jit(solution)/shard_map/ppermute | solution.py:25
  37.7 1.9 %collective-permute-start.2 = (bf16[64,2048]{1,0:T(8,128)(2,1)}, bf16[64,2048]{1,0:T(8,128)(2,1)}, u32[]{:S(2)}, u32[]{:S(2)}) collective-permute-start(bf16[64,2048]{1,0:T(8,128)(2,1)} %get-tuple-element.25), channel_id=1, source_target_pairs={{0,12},{4,0},{8,4},{12,8},{1,13},{5,1},{9,5},{13,9},{2,14},{6,2},{... | collective-permute-start | bytes 786440 | tf_op jit(solution)/shard_map/ppermute | solution.py:25
  39.6 5.1 %collective-permute-start.3 = (bf16[64,2048]{1,0:T(8,128)(2,1)}, bf16[64,2048]{1,0:T(8,128)(2,1)}, u32[]{:S(2)}, u32[]{:S(2)}) collective-permute-start(bf16[64,2048]{1,0:T(8,128)(2,1)} %get-tuple-element.24), channel_id=1, source_target_pairs={{0,4},{4,8},{8,12},{12,0},{1,5},{5,9},{9,13},{13,1},{2,6},{6,10},{... | collective-permute-start | bytes 786440 | tf_op jit(solution)/shard_map/ppermute | solution.py:25
  44.7 0.0 all-to-all-done.1
  44.8 0.0 copy-start.1
  44.8 0.8 shard_map.46
  45.6 0.0 copy-done.1
  45.6 3.4 %all-to-all-start.2 = ((bf16[8,32,512]{2,1,0:T(8,128)(2,1)}), bf16[8,32,512]{2,1,0:T(8,128)(2,1)S(1)}, u32[]{:S(2)}, u32[]{:S(2)}) async-start(bf16[8,32,512]{2,1,0:T(8,128)(2,1)} %shard_map.46), calls=%async_computation.2 | async-start | bytes 524288 | tf_op jit(solution)/shard_map/all_to_all | solution.py:15
  49.0 0.0 collective-permute-done.1
  49.0 0.3 collective-permute-done.2
  49.3 0.0 collective-permute-done.3
  49.3 1.3 %fusion.8 = bf16[64,2048]{1,0:T(8,128)(2,1)S(1)} fusion(bf16[64,2048]{1,0:T(8,128)(2,1)} %collective-permute-done.3, bf16[64,2048]{1,0:T(8,128)(2,1)} %collective-permute-done.2, bf16[64,2048]{1,0:T(8,128)(2,1)} %collective-permute-done.1, bf16[4,64,2048]{2,1,0:T(8,128)(2,1)} %bitcast.39, s32[]{:T(128)S(6)} %select_n.48), kind=kLoop, calls=%fused_computation.8 | loop fusion | flops 1048576 | bytes 1310724 | tf_op jit(solution)/shard_map/convert_element_type | solution.py:150
  50.6 0.7 dynamic-slice_bitcast_fusion.3
  51.4 3.4 %collective-permute-start.4 = (bf16[32,2048]{1,0:T(8,128)(2,1)}, bf16[32,2048]{1,0:T(8,128)(2,1)}, u32[]{:S(2)}, u32[]{:S(2)}) collective-permute-start(bf16[32,2048]{1,0:T(8,128)(2,1)} %get-tuple-element.26), channel_id=1, source_target_pairs={{0,1},{1,0},{2,3},{3,2},{4,5},{5,4},{6,7},{7,6},{8,9},{9,8},{10,11... | collective-permute-start | bytes 393224 | tf_op jit(solution)/shard_map/ppermute | solution.py:25
  54.7 5.6 %all-to-all-done.2 = bf16[8,32,512]{2,1,0:T(8,128)(2,1)S(1)} async-done(((bf16[8,32,512]{2,1,0:T(8,128)(2,1)}), bf16[8,32,512]{2,1,0:T(8,128)(2,1)S(1)}, u32[]{:S(2)}, u32[]{:S(2)}) %all-to-all-start.2) | async-done | bytes 262176 | tf_op jit(solution)/shard_map/all_to_all | solution.py:15
  60.3 3.2 %shard_map.47 = bf16[256,2048]{1,0:T(8,128)(2,1)} custom-call(bf16[256,512]{1,0:T(8,128)(2,1)S(1)} %bitcast.37, bf16[2048,512]{1,0:T(8,128)(2,1)} %bitcast.45), custom_call_target="tpu_custom_call" | custom-call | flops 199999995904 | bytes 1048576 | tf_op jit(solution)/shard_map/pallas_call | solution.py:111
  63.5 0.0 copy-start.4
  63.5 0.0 collective-permute-done.4
  63.5 5.6 %all-to-all-start.3 = ((bf16[8,32,2048]{2,1,0:T(8,128)(2,1)}), bf16[8,32,2048]{2,1,0:T(8,128)(2,1)S(1)}, u32[]{:S(2)}, u32[]{:S(2)}) async-start(bf16[8,32,2048]{2,1,0:T(8,128)(2,1)} %bitcast.16), calls=%async_computation.3 | async-start | bytes 2097152 | tf_op jit(solution)/shard_map/all_to_all | solution.py:15
  69.1 0.0 copy-done.4
  69.1 0.9 add_convert_fusion
  70.0 4.3 %collective-permute-start.5 = (bf16[32,2048]{1,0:T(8,128)(2,1)S(1)}, bf16[32,2048]{1,0:T(8,128)(2,1)S(1)}, u32[]{:S(2)}, u32[]{:S(2)}) collective-permute-start(bf16[32,2048]{1,0:T(8,128)(2,1)S(1)} %add_convert_fusion), channel_id=1, source_target_pairs={{0,2},{2,0},{1,3},{3,1},{4,6},{6,4},{5,7},{7,5},{8,10},{10,8},{9,1... | collective-permute-start | bytes 393224 | tf_op jit(solution)/shard_map/ppermute | solution.py:25
  74.3 9.4 %all-to-all-done.3 = bf16[8,32,2048]{2,1,0:T(8,128)(2,1)S(1)} async-done(((bf16[8,32,2048]{2,1,0:T(8,128)(2,1)}), bf16[8,32,2048]{2,1,0:T(8,128)(2,1)S(1)}, u32[]{:S(2)}, u32[]{:S(2)}) %all-to-all-start.3) | async-done | bytes 1048608 | tf_op jit(solution)/shard_map/all_to_all | solution.py:15
  83.7 0.1 reduce_sum.21
  83.8 0.0 collective-permute-done.5
  83.8 2.6 %collective-permute-start.6 = (bf16[32,2048]{1,0:T(8,128)(2,1)S(1)}, bf16[32,2048]{1,0:T(8,128)(2,1)S(1)}, u32[]{:S(2)}, u32[]{:S(2)}) collective-permute-start(bf16[32,2048]{1,0:T(8,128)(2,1)S(1)} %reduce_sum.21), channel_id=1, source_target_pairs={{0,2},{2,0},{1,3},{3,1},{4,6},{6,4},{5,7},{7,5},{8,10},{10,8},{9,1... | collective-permute-start | bytes 393224 | tf_op jit(solution)/shard_map/ppermute | solution.py:25
  86.4 0.2 fusion.13
  86.6 6.4 %collective-permute-done.6 = bf16[32,2048]{1,0:T(8,128)(2,1)S(1)} collective-permute-done((bf16[32,2048]{1,0:T(8,128)(2,1)S(1)}, bf16[32,2048]{1,0:T(8,128)(2,1)S(1)}, u32[]{:S(2)}, u32[]{:S(2)}) %collective-permute-start.6) | collective-permute-done | bytes 131104 | tf_op jit(solution)/shard_map/ppermute | solution.py:25
  93.0 0.1 broadcast_in_dim.18
  93.2 13.5 %all_to_all.30 = bf16[8,32,2048]{2,1,0:T(8,128)(2,1)S(1)} all-to-all(bf16[8,32,2048]{2,1,0:T(8,128)(2,1)S(1)} %broadcast_in_dim.18), channel_id=1, replica_groups=mesh['section'=4,'dp'=8,'tx'=4,'ty1'=2,'ty0'=2] {'tx','ty0'}, dimensions={0} | all-to-all | bytes 2097152 | tf_op jit(solution)/shard_map/all_to_all | solution.py:15
  106.6 0.0 copy-start.2
  106.7 0.7 fusion.3
  107.4 14.2 %all_to_all.31 = bf16[8,32,512]{2,1,0:T(8,128)(2,1)S(1)} all-to-all(bf16[8,32,512]{2,1,0:T(8,128)(2,1)S(1)} %bitcast.43), channel_id=1, replica_groups=mesh['section'=4,'dp'=8,'tx'=4,'ty1'=2,'ty0'=2] {'dp'}, dimensions={0} | all-to-all | bytes 524288 | tf_op jit(solution)/shard_map/all_to_all | solution.py:15
  121.7 0.0 copy-done.2
  121.7 0.6 fusion.14
  (3 shorter events, 0.1 us)
Async XLA Ops:
  0.0 31.7 %copy-start = (bf16[1,512,2048]{2,1,0:T(8,128)(2,1)S(1)}, bf16[1,512,2048]{2,1,0:T(8,128)(2,1)}, u32[]{:S(2)}) copy-start(bf16[1,512,2048]{2,1,0:T(8,128)(2,1)} %param.5) | copy-start | bytes 6291460
  1.6 22.2 %all-to-all-start = ((bf16[8,32,512]{2,1,0:T(8,128)(2,1)}), bf16[8,32,512]{2,1,0:T(8,128)(2,1)S(1)}, u32[]{:S(2)}, u32[]{:S(2)}) async-start(bf16[8,32,512]{2,1,0:T(8,128)(2,1)} %broadcast_in_dim.17), calls=%async_computation | async-start | bytes 524288 | tf_op jit(solution)/shard_map/all_to_all | solution.py:15
  11.9 8.8 %collective-permute-start = (bf16[2,8192]{1,0:T(2,128)(2,1)}, bf16[2,8192]{1,0:T(2,128)(2,1)}, u32[]{:S(2)}, u32[]{:S(2)}) collective-permute-start(bf16[2,8192]{1,0:T(2,128)(2,1)} %bitcast.46), channel_id=1, source_target_pairs={{0,384},{128,0},{256,128},{384,256},{1,385},{129,1},{257,129},{385... | collective-permute-start | bytes 98312 | tf_op jit(solution)/shard_map/ppermute | solution.py:25
  23.8 20.9 %all-to-all-start.1 = ((bf16[16,2,512]{2,1,0:T(2,128)(2,1)}), bf16[16,2,512]{2,1,0:T(2,128)(2,1)S(1)}, u32[]{:S(2)}, u32[]{:S(2)}) async-start(bf16[16,2,512]{2,1,0:T(2,128)(2,1)} %bitcast.4), calls=%async_computation.1 | async-start | bytes 65536 | tf_op jit(solution)/shard_map/all_to_all | solution.py:15
  32.4 1.0 copy-start.3
  34.3 14.7 %collective-permute-start.1 = (bf16[64,2048]{1,0:T(8,128)(2,1)}, bf16[64,2048]{1,0:T(8,128)(2,1)}, u32[]{:S(2)}, u32[]{:S(2)}) collective-permute-start(bf16[64,2048]{1,0:T(8,128)(2,1)} %get-tuple-element.23), channel_id=1, source_target_pairs={{0,8},{4,12},{8,0},{12,4},{1,9},{5,13},{9,1},{13,5},{2,10},{6,14},... | collective-permute-start | bytes 786440 | tf_op jit(solution)/shard_map/ppermute | solution.py:25
  37.7 11.7 %collective-permute-start.2 = (bf16[64,2048]{1,0:T(8,128)(2,1)}, bf16[64,2048]{1,0:T(8,128)(2,1)}, u32[]{:S(2)}, u32[]{:S(2)}) collective-permute-start(bf16[64,2048]{1,0:T(8,128)(2,1)} %get-tuple-element.25), channel_id=1, source_target_pairs={{0,12},{4,0},{8,4},{12,8},{1,13},{5,1},{9,5},{13,9},{2,14},{6,2},{... | collective-permute-start | bytes 786440 | tf_op jit(solution)/shard_map/ppermute | solution.py:25
  39.6 9.7 %collective-permute-start.3 = (bf16[64,2048]{1,0:T(8,128)(2,1)}, bf16[64,2048]{1,0:T(8,128)(2,1)}, u32[]{:S(2)}, u32[]{:S(2)}) collective-permute-start(bf16[64,2048]{1,0:T(8,128)(2,1)} %get-tuple-element.24), channel_id=1, source_target_pairs={{0,4},{4,8},{8,12},{12,0},{1,5},{5,9},{9,13},{13,1},{2,6},{6,10},{... | collective-permute-start | bytes 786440 | tf_op jit(solution)/shard_map/ppermute | solution.py:25
  44.8 0.8 copy-start.1
  45.6 14.7 %all-to-all-start.2 = ((bf16[8,32,512]{2,1,0:T(8,128)(2,1)}), bf16[8,32,512]{2,1,0:T(8,128)(2,1)S(1)}, u32[]{:S(2)}, u32[]{:S(2)}) async-start(bf16[8,32,512]{2,1,0:T(8,128)(2,1)} %shard_map.46), calls=%async_computation.2 | async-start | bytes 524288 | tf_op jit(solution)/shard_map/all_to_all | solution.py:15
  51.4 12.2 %collective-permute-start.4 = (bf16[32,2048]{1,0:T(8,128)(2,1)}, bf16[32,2048]{1,0:T(8,128)(2,1)}, u32[]{:S(2)}, u32[]{:S(2)}) collective-permute-start(bf16[32,2048]{1,0:T(8,128)(2,1)} %get-tuple-element.26), channel_id=1, source_target_pairs={{0,1},{1,0},{2,3},{3,2},{4,5},{5,4},{6,7},{7,6},{8,9},{9,8},{10,11... | collective-permute-start | bytes 393224 | tf_op jit(solution)/shard_map/ppermute | solution.py:25
  63.5 5.6 %copy-start.4 = (bf16[32,2048]{1,0:T(8,128)(2,1)S(1)}, bf16[32,2048]{1,0:T(8,128)(2,1)}, u32[]{:S(2)}) copy-start(bf16[32,2048]{1,0:T(8,128)(2,1)} %get-tuple-element.17) | copy-start | bytes 393220
  63.5 20.1 %all-to-all-start.3 = ((bf16[8,32,2048]{2,1,0:T(8,128)(2,1)}), bf16[8,32,2048]{2,1,0:T(8,128)(2,1)S(1)}, u32[]{:S(2)}, u32[]{:S(2)}) async-start(bf16[8,32,2048]{2,1,0:T(8,128)(2,1)} %bitcast.16), calls=%async_computation.3 | async-start | bytes 2097152 | tf_op jit(solution)/shard_map/all_to_all | solution.py:15
  70.0 13.8 %collective-permute-start.5 = (bf16[32,2048]{1,0:T(8,128)(2,1)S(1)}, bf16[32,2048]{1,0:T(8,128)(2,1)S(1)}, u32[]{:S(2)}, u32[]{:S(2)}) collective-permute-start(bf16[32,2048]{1,0:T(8,128)(2,1)S(1)} %add_convert_fusion), channel_id=1, source_target_pairs={{0,2},{2,0},{1,3},{3,1},{4,6},{6,4},{5,7},{7,5},{8,10},{10,8},{9,1... | collective-permute-start | bytes 393224 | tf_op jit(solution)/shard_map/ppermute | solution.py:25
  83.8 9.2 %collective-permute-start.6 = (bf16[32,2048]{1,0:T(8,128)(2,1)S(1)}, bf16[32,2048]{1,0:T(8,128)(2,1)S(1)}, u32[]{:S(2)}, u32[]{:S(2)}) collective-permute-start(bf16[32,2048]{1,0:T(8,128)(2,1)S(1)} %reduce_sum.21), channel_id=1, source_target_pairs={{0,2},{2,0},{1,3},{3,1},{4,6},{6,4},{5,7},{7,5},{8,10},{10,8},{9,1... | collective-permute-start | bytes 393224 | tf_op jit(solution)/shard_map/ppermute | solution.py:25
  106.6 15.0 %copy-start.2 = (bf16[32,512]{1,0:T(8,128)(2,1)S(1)}, bf16[32,512]{1,0:T(8,128)(2,1)}, u32[]{:S(2)}) copy-start(bf16[32,512]{1,0:T(8,128)(2,1)} %copy-done.1) | copy-start | bytes 98308
